TPU v7x, 256 devices: a whole 4x4x8 slice. The times are simulated.
256 devices in a mesh: layer: 4 (over y), strip: 8 (over x, core), dir: 8 (over z).
Axes of the slice: x: 4, y: 4, z: 8, core: 2. Of those that a mesh axis runs over, the one named last changes fastest.
Arguments:
- screen: float32 [4, 2048, 4096], P('layer', 'strip', 'dir'), may hold values from -6 to 6
- innovation: bfloat16 [3, 4, 2048, 4096], P(None, 'layer', 'strip', 'dir'), may hold values from -6 to 6
- coef: float32 [4, 5, 4096], P('layer', None, 'dir'), may hold values from -2 to 2
- wind: int32 [4], P('layer'), may hold values from -2 to 2
- row_blocks: int32 [8, 4, 32], P(None, 'layer'), may hold values from 0 to 127, as said below
- table_index: int32 [8, 4], P(None, 'layer'), may hold values from 0 to 1
- row_table: bfloat16 [2, 512, 512], replicated, may hold values from -0.125 to 0.125
- column_table: bfloat16 [2, 512, 4096], P(None, None, 'dir'), may hold values from -0.09375 to 0.09375
Outputs:
- screen_out: float32 [4, 2048, 4096], P('layer', 'strip', 'dir')
- slopes: float32 [3, 2, 512, 8, 512], P(None, None, ('layer', 'strip'), 'dir')
Inputs may be any that keep to these rules, and one draw needn't show every extreme that they name: `row_blocks`: for each direction and layer, 32 consecutive row blocks counted modulo 128.
All inputs are finite; a program needn't handle non-finite values.
Results may differ from a plain program's by a relative error of at most 0.0029.
Values sent between devices are 32-bit elements; how exact they have to be, the bound alone decides.
No kernel may reach another device: no remote copies, remote signals or barrier semaphores. Data moves between devices by JAX's collectives and lax.ppermute only.
A program may use at most 128 MiB of HBM per device.

v0:
```python
import jax
import jax.numpy as jnp
from jax import lax
from jax.experimental import pallas as pl
from jax.experimental.pallas import tpu as pltpu
from jax.sharding import PartitionSpec as P

ROWS = 256
COLS = 512
PR = 512
PC = 512
STEPS = 3
NM = 2
NDIR = 8
LAYERS = 4
STRIPS = 8
TAPS = 5
CHUNKS = LAYERS * STRIPS
PAD = 16
LANES = 128
GROUP = STEPS * 2 * 8
PLANE = ("layer", "strip")


def advance(window, fresh, coef, shift):
    count = fresh.shape[0]
    moved = pltpu.roll(window, shift, axis=0)
    total = fresh.astype(jnp.float32)
    for k in range(TAPS):
        total = total + coef[k] * moved[8 + k : 8 + k + count, :]
    return total


def inner_kernel(
    wind, screen, fresh, coef, column_table, flats, near0, fresh0, near1, near2, near3, table, taps, s3, s1, s2
):
    shift = wind[0] + 2
    table[...] = column_table[...]
    taps[...] = coef[...]
    near0[0] = screen[0:16, :]
    near0[1] = screen[ROWS - 16 : ROWS, :]
    fresh0[0] = fresh[:, 0:32, :]
    fresh0[1] = fresh[:, ROWS - 32 : ROWS, :]
    steps = ((screen, s1, near1, 16, 16), (s1, s2, near2, 16, 16), (s2, s3, near3, 8, 32))
    for t, (src, dst, near, count, flat) in enumerate(steps):
        begin, end = 8 * (t + 1), ROWS - 8 * (t + 1)
        for r in range(begin, end, 32):
            stop = min(r + 32, end)
            dst[r:stop, :] = advance(src[r - 8 : stop + 8, :], fresh[t, r:stop, :], coef, shift)
        near[0:count, :] = dst[begin : begin + count, :]
        near[count:, :] = dst[end - count : end, :]
        for r in range(flat, ROWS - flat, 32):
            stop = min(r + 32, ROWS - flat)
            flats[t, r:stop, :] = dst[r:stop, :].astype(jnp.bfloat16)


def outer_kernel(
    wind,
    near0,
    fresh0,
    low,
    high,
    coef,
    near1,
    near2,
    near3,
    table,
    inside,
    old,
    images,
    screen_out,
    flat,
    piece,
    ends,
    sem,
):
    shift = wind[0] + 2
    none = jnp.zeros((8, COLS), jnp.float32)
    join = lambda *rows: jnp.concatenate(rows, axis=0)
    after = lambda window, fresh: advance(window, fresh, coef, shift)
    def project(t):
        for m in range(NM):
            image = lax.dot_general(
                table[m], flat[t], (((1,), (1,)), ((), ())), preferred_element_type=jnp.float32
            )
            for half in range(2):
                for part in range(2):
                    at = image[half * 256 : half * 256 + 256, part * LANES : part * LANES + LANES]
                    piece[t, :, part, m, half, :, :] = at.reshape(CHUNKS, 8, LANES)
        copy = pltpu.make_async_copy(piece.at[t], images.at[:, :, t], sem.at[t])
        copy.start()
        return copy

    first, final = fresh0[0, 0].astype(jnp.float32), fresh0[1, 0].astype(jnp.float32)
    e = after(join(low[0:16, :], near0[0]), join(low[16:24, :], first[0:8]))
    f = after(join(near0[1], high[0:16, :]), join(final[24:32], high[16:24, :]))
    flat[0] = inside[0]
    flat[0, 0:16, :] = join(e[8:16], near1[0:8, :]).astype(jnp.bfloat16)
    flat[0, ROWS - 16 : ROWS, :] = join(near1[24:32, :], f[0:8]).astype(jnp.bfloat16)
    leave = [project(0)]

    first, final = fresh0[0, 1].astype(jnp.float32), fresh0[1, 1].astype(jnp.float32)
    e = after(join(none, e, near1[0:16, :]), join(low[24:32, :], first[0:16]))
    f = after(join(near1[16:32, :], f, none), join(final[16:32], high[24:32, :]))
    flat[1] = inside[1]
    flat[1, 0:16, :] = e[8:24].astype(jnp.bfloat16)
    flat[1, ROWS - 16 : ROWS, :] = f[0:16].astype(jnp.bfloat16)
    leave.append(project(1))

    first, final = fresh0[0, 2].astype(jnp.float32), fresh0[1, 2].astype(jnp.float32)
    e = after(join(e, near2[0:16, :]), first[0:24])
    f = after(join(near2[16:32, :], f), final[8:32])
    ends[0] = e
    ends[1] = f
    leave += [
        pltpu.make_async_copy(ends.at[0], screen_out.at[pl.ds(0, 24), :], sem.at[3]),
        pltpu.make_async_copy(ends.at[1], screen_out.at[pl.ds(ROWS - 24, 24), :], sem.at[4]),
    ]
    leave[-2].start()
    leave[-1].start()
    flat[2] = inside[2]
    flat[2, 0:32, :] = join(e, near3[0:8, :]).astype(jnp.bfloat16)
    flat[2, ROWS - 32 : ROWS, :] = join(near3[8:16, :], f).astype(jnp.bfloat16)
    leave.append(project(2))
    for copy in leave:
        copy.wait()


def pupil_kernel(mine, places, x, table, *refs):
    *outs, feet, pupils = refs
    feet[...] = jnp.zeros(feet.shape, jnp.float32)
    lane = lax.broadcasted_iota(jnp.int32, (GROUP, LANES), 1)

    for layer in range(LAYERS):
        for d in range(NDIR):
            start = places[layer * 2 * NDIR + d]
            m = places[(layer * 2 + 1) * NDIR + d]
            block = start // 8
            shift = (start % 8) * 16
            back = (LANES - shift) % LANES
            rolled = []
            for i in range(5):
                rows = x[layer * 16 + (block + i) % 16, :, m]
                rolled.append(pltpu.roll(rows.reshape(GROUP, LANES), back, axis=1))
            for i in range(4):
                piece = jnp.where(lane < LANES - shift, rolled[i], rolled[i + 1])
                at = (m, pl.ds(d * GROUP, GROUP), pl.ds(i * LANES, LANES))
                feet[at] = feet[at] + piece

    total = None
    for m in range(NM):
        whole = feet[m]
        head = whole.astype(jnp.bfloat16)
        tail = (whole - head.astype(jnp.float32)).astype(jnp.bfloat16)
        for part in (head, tail):
            product = lax.dot_general(
                part, table[m], (((1,), (1,)), ((), ())), preferred_element_type=jnp.float32
            )
            total = product if total is None else total + product
    pupils[...] = total.reshape(pupils.shape)
    for j, out in enumerate(outs):
        out[...] = pupils[(mine[0] + j) % NDIR]


def pack_kernel(x, y, z, out):
    total = x[...] + y[...] + z[...]
    tiles = [total[8 * j : 8 * j + 8] for j in range(6)]

    lane = lax.broadcasted_iota(jnp.int32, (8, LANES), 1)
    slot = lane // 16
    within = lane % 16
    heads = []
    for g in range(4):
        gathered = tiles[0][:, g * LANES : g * LANES + LANES]
        for j in range(1, 6):
            moved = pltpu.roll(tiles[j][:, g * LANES : g * LANES + LANES], j, axis=1)
            gathered = jnp.where(within == j, moved, gathered)
        heads.append(gathered)
    for g in range(4):
        for q in range(8):
            if q < 7:
                packed = pltpu.roll(heads[g], (96 - 16 * (q + 1)) % LANES, axis=1)
            elif g < 3:
                packed = pltpu.roll(heads[g + 1], 96, axis=1)
            else:
                packed = jnp.zeros((8, LANES), jnp.float32)
            for j in range(6):
                turn = (16 * j - 16 * q) % LANES
                moved = tiles[j][:, g * LANES : g * LANES + LANES]
                moved = moved if turn == 0 else pltpu.roll(moved, turn, axis=1)
                packed = jnp.where(slot == j, moved, packed)
            out[g * 8 + q] = packed


def slope_kernel(x, out):
    flipped = jnp.transpose(x[...].reshape(CHUNKS * 8, LANES))
    for t in range(STEPS):
        left = flipped[32 * t : 32 * t + 16]
        right = flipped[32 * t + 16 : 32 * t + 32]
        rows = jnp.concatenate([left, right], axis=1)
        edge = jnp.concatenate(
            [flipped[96 + 2 * t : 97 + 2 * t], flipped[97 + 2 * t : 98 + 2 * t]], axis=1
        )
        beside = jnp.concatenate([rows[:, 1:], jnp.zeros((16, 1), jnp.float32)], axis=1)
        below = jnp.concatenate([rows[1:], edge], axis=0)
        out[t, 0] = (beside - rows).reshape(16, 1, PC)
        out[t, 1] = (below - rows).reshape(16, 1, PC)


def neighbours(count, by):
    return [(i, (i + by) % count) for i in range(count)]


SCALARS = pl.BlockSpec(memory_space=pltpu.SMEM)


def room(mib):
    return pltpu.CompilerParams(vmem_limit_bytes=int(mib * 1024 * 1024))


def whole(*shape):
    return pl.BlockSpec(shape, lambda *_: (0,) * len(shape))


def shards(screen, innovation, coef, wind, row_blocks, table_index, row_table, column_table):
    state = screen[0]
    fresh = innovation[:, 0]
    taps = jnp.swapaxes(coef, 0, 1)
    strips = lax.axis_size("strip")

    last = [state[-16:], fresh[0, -8:].astype(jnp.float32), fresh[1, -8:].astype(jnp.float32)]
    begin = [state[:16], fresh[0, :8].astype(jnp.float32), fresh[1, :8].astype(jnp.float32)]
    low = lax.ppermute(jnp.concatenate(last, axis=0), "strip", neighbours(strips, 1))
    high = lax.ppermute(jnp.concatenate(begin, axis=0), "strip", neighbours(strips, -1))

    near = jax.ShapeDtypeStruct((32, COLS), jnp.float32)
    *inside, unfinished = pl.pallas_call(
        inner_kernel,
        in_specs=[
            SCALARS,
            whole(ROWS, COLS),
            whole(STEPS, ROWS, COLS),
            whole(TAPS, 1, COLS),
            whole(NM, PC, COLS),
        ],
        out_specs=[
            whole(STEPS, ROWS, COLS),
            whole(2, 16, COLS),
            whole(2, STEPS, 32, COLS),
            whole(32, COLS),
            whole(32, COLS),
            whole(16, COLS),
            whole(NM, PC, COLS),
            whole(TAPS, 1, COLS),
            whole(ROWS, COLS),
        ],
        out_shape=[
            jax.ShapeDtypeStruct((STEPS, ROWS, COLS), jnp.bfloat16),
            jax.ShapeDtypeStruct((2, 16, COLS), jnp.float32),
            jax.ShapeDtypeStruct((2, STEPS, 32, COLS), jnp.bfloat16),
            near,
            near,
            jax.ShapeDtypeStruct((16, COLS), jnp.float32),
            jax.ShapeDtypeStruct((NM, PC, COLS), jnp.bfloat16),
            jax.ShapeDtypeStruct((TAPS, 1, COLS), jnp.float32),
            jax.ShapeDtypeStruct((ROWS, COLS), jnp.float32),
        ],
        scratch_shapes=[pltpu.VMEM((ROWS, COLS), jnp.float32)] * 2,
        compiler_params=room(50),
        cost_estimate=pl.CostEstimate(
            flops=12 * STEPS * ROWS * COLS, bytes_accessed=14 * ROWS * COLS, transcendentals=0
        ),
        name="inner",
    )(wind, state, fresh, taps, column_table)

    anywhere = pl.BlockSpec(memory_space=pl.ANY)
    images, screen_out = pl.pallas_call(
        outer_kernel,
        in_specs=[
            SCALARS,
            whole(2, 16, COLS),
            whole(2, STEPS, 32, COLS),
            whole(32, COLS),
            whole(32, COLS),
            whole(TAPS, 1, COLS),
            whole(32, COLS),
            whole(32, COLS),
            whole(16, COLS),
            whole(NM, PC, COLS),
            whole(STEPS, ROWS, COLS),
            anywhere,
        ],
        out_specs=[anywhere, anywhere],
        out_shape=[
            jax.ShapeDtypeStruct((CHUNKS, 2, STEPS, NM, 2, 8, LANES), jnp.float32),
            jax.ShapeDtypeStruct((ROWS, COLS), jnp.float32),
        ],
        input_output_aliases={11: 1},
        scratch_shapes=[
            pltpu.VMEM((STEPS, ROWS, COLS), jnp.bfloat16),
            pltpu.VMEM((STEPS, CHUNKS, 2, NM, 2, 8, LANES), jnp.float32),
            pltpu.VMEM((2, 24, COLS), jnp.float32),
            pltpu.SemaphoreType.DMA((5,)),
        ],
        compiler_params=room(50),
        name="outer",
    )(
        wind,
        *inside[1:3],
        low,
        high,
        inside[7],
        *inside[3:7],
        inside[0],
        unfinished,
    )

    gathered = lax.all_to_all(images, PLANE, 0, 0, tiled=True)
    places = jnp.stack([row_blocks[:, 0, 0], table_index[:, 0]])
    places = lax.all_gather(places, "layer").reshape(LAYERS * 2 * NDIR)
    mine = lax.axis_index("dir").astype(jnp.int32).reshape(1)
    pupils = pl.pallas_call(
        pupil_kernel,
        in_specs=[
            SCALARS,
            SCALARS,
            whole(CHUNKS * 2, STEPS, NM, 2, 8, LANES),
            whole(NM, PR, PR),
        ],
        out_specs=[whole(GROUP, PR)] * NDIR,
        out_shape=[jax.ShapeDtypeStruct((GROUP, PR), jnp.float32)] * NDIR,
        scratch_shapes=[
            pltpu.VMEM((NM, NDIR * GROUP, PR), jnp.float32),
            pltpu.VMEM((NDIR, GROUP, PR), jnp.float32),
        ],
        compiler_params=room(24),
        name="pupil",
    )(mine, places, gathered.reshape(CHUNKS * 2, STEPS, NM, 2, 8, LANES), row_table)

    count = lax.axis_size("dir")
    up = lambda x: lax.ppermute(x, "dir", neighbours(count, 1))
    down = lambda x: lax.ppermute(x, "dir", neighbours(count, -1))
    rising = up(pupils[4])
    falling = down(pupils[5])
    rising = up(pupils[3] + rising)
    falling = down(pupils[6] + falling)
    rising = up(pupils[2] + rising)
    falling = down(pupils[7] + falling)
    rising = up(pupils[1] + rising)
    packed = pl.pallas_call(
        pack_kernel,
        in_specs=[whole(GROUP, PR)] * 3,
        out_specs=whole(CHUNKS, 8, LANES),
        out_shape=jax.ShapeDtypeStruct((CHUNKS, 8, LANES), jnp.float32),
        compiler_params=room(16),
        name="pack",
    )(pupils[0], rising, falling)
    rows = lax.all_to_all(packed, PLANE, 0, 0, tiled=True)
    slopes = pl.pallas_call(
        slope_kernel,
        in_specs=[whole(CHUNKS, 8, LANES)],
        out_specs=whole(STEPS, 2, 16, 1, PC),
        out_shape=jax.ShapeDtypeStruct((STEPS, 2, 16, 1, PC), jnp.float32),
        compiler_params=room(16),
        name="slopes",
    )(rows)
    return (screen_out[None], slopes)


def solution(mesh):
    return jax.shard_map(
        shards,
        mesh=mesh,
        in_specs=(
            P("layer", "strip", "dir"),
            P(None, "layer", "strip", "dir"),
            P("layer", None, "dir"),
            P("layer"),
            P(None, "layer", None),
            P(None, "layer"),
            P(),
            P(None, None, "dir"),
        ),
        out_specs=(P("layer", "strip", "dir"), P(None, None, ("layer", "strip"), "dir", None)),
        check_vma=False,
    )
```

profile of v0, /device:TPU:1, one launch (start us, length us, event | category | flops | bytes accessed | tf_op | source)
XLA Modules:
  0.0 106.6 jit_solution(6258635627040222523)
XLA Ops:
  0.6 0.8 fusion.1
  1.4 0.8 slice_bitcast_fusion
  2.2 2.6 %collective-permute-start = (f32[32,512]{1,0:T(8,128)S(1)}, f32[32,512]{1,0:T(8,128)S(1)}, u32[]{:S(2)}, u32[]{:S(2)}) collective-permute-start(f32[32,512]{1,0:T(8,128)S(1)} %pad_maximum_fusion), channel_id=1, source_target_pairs={{0,8},{8,16},{16,24},{24,32},{32,40},{40,48},{48,56},{56,0},{1,9},... | collective-permute-start | bytes 196616 | tf_op jit(solution)/shard_map/ppermute | solution.py:233
  4.8 0.7 collective-permute-start.1
  6.1 0.0 copy-start.1
  6.1 1.1 %copy-done.1 = bf16[3,1,256,512]{3,2,1,0:T(8,128)(2,1)S(1)} copy-done((bf16[3,1,256,512]{3,2,1,0:T(8,128)(2,1)S(1)}, bf16[3,1,256,512]{3,2,1,0:T(8,128)(2,1)}, u32[]{:S(2)}) %copy-start.1) | copy-done | bytes 786456
  7.3 1.0 copy-done.2
  8.3 0.7 copy-done.3
  9.0 3.4 %inner.1 = (bf16[3,256,512]{2,1,0:T(8,128)(2,1)S(1)}, f32[2,16,512]{2,1,0:T(8,128)S(1)}, bf16[2,3,32,512]{3,2,1,0:T(8,128)(2,1)S(1)}, f32[32,512]{1,0:T(8,128)S(...) custom-call(s32[1]{0:T(128)S(6)} %copy.12.wind, ...), custom_call_target="tpu_custom_call" | custom-call | flops 4718592 | bytes 1835008 | tf_op jit(solution)/shard_map/inner/pallas_call | solution.py:237
  12.4 2.3 %outer.1 = (f32[32,2,3,2,2,8,128]{6,5,4,3,2,1,0:T(8,128)}, f32[256,512]{1,0:T(8,128)}) custom-call(s32[1]{0:T(128)S(6)} %copy.12.wind, f32[2,16,512]{2,1,0:T(8,128)S(1)} %get-tuple-element.21.near0, bf16[2,3,32,512]{3,2,1,0:T(8,128)(2,1)S(1)} %get-tuple-element.22.fresh0, f32[32,512]{1,0:T(8,128)S(1)} %collective-permute-done.low, ...), custom_call_target="tpu_custom_call", output_to_operand_aliasing={{1}: (11, {})} | custom-call | tf_op jit(solution)/shard_map/outer/pallas_call | solution.py:277
  14.7 0.0 copy-start.4
  14.7 7.1 %all-to-all-start = ((f32[32,2,3,2,2,8,128]{6,5,4,3,2,1,0:T(8,128)}), f32[32,2,3,2,2,8,128]{6,5,4,3,2,1,0:T(8,128)S(1)}, u32[]{:S(2)}, u32[]{:S(2)}) async-start(f32[32,2,3,2,2,8,128]{6,5,4,3,2,1,0:T(8,128)} %get-tuple-element.31), calls=%async_computation | async-start | bytes 6291456 | tf_op jit(solution)/shard_map/all_to_all | solution.py:318
  21.8 0.2 slice_reduce_fusion
  22.1 36.4 %all-gather.1 = s32[4,2,8]{2,1,0:T(2,128)S(1)} all-gather(s32[1,2,8]{2,1,0:T(2,128)S(1)} %add_bitcast_fusion), channel_id=2, replica_groups=mesh['layer'=4,'strip'=8,'dir'=8] {'layer'}, dimensions={0}, use_global_device_ids=true | all-gather | bytes 320 | tf_op jit(solution)/shard_map/all_gather | solution.py:320
  58.5 0.1 reshape.24.places
  58.6 2.4 %all-to-all-done = f32[32,2,3,2,2,8,128]{6,5,4,3,2,1,0:T(8,128)S(1)} async-done(((f32[32,2,3,2,2,8,128]{6,5,4,3,2,1,0:T(8,128)}), f32[32,2,3,2,2,8,128]{6,5,4,3,2,1,0:T(8,128)S(1)}, u32[]{:S(2)}, u32[]{:S(2)}) %all-to-all-start) | async-done | bytes 3145760 | tf_op jit(solution)/shard_map/all_to_all | solution.py:318
  61.0 1.2 %copy-done = bf16[2,512,512]{2,1,0:T(8,128)(2,1)S(1)} copy-done((bf16[2,512,512]{2,1,0:T(8,128)(2,1)S(1)}, bf16[2,512,512]{2,1,0:T(8,128)(2,1)}, u32[]{:S(2)}) %copy-start) | copy-done | bytes 1048600
  62.2 2.7 %pupil.1 = (f32[48,512]{1,0:T(8,128)S(1)}, f32[48,512]{1,0:T(8,128)S(1)}, f32[48,512]{1,0:T(8,128)S(1)}, f32[48,512]{1,0:T(8,128)S(1)}, f32[48,512]{1,0:T(8,128)...) custom-call(s32[1]{0:T(128)} %bitcast.10.mine, s32[64]{0:T(128)S(1)} %reshape.24.places, ...), custom_call_target="tpu_custom_call" | custom-call | tf_op jit(solution)/shard_map/pupil/pallas_call | solution.py:322
  64.9 1.7 %collective-permute-start.2 = (f32[48,512]{1,0:T(8,128)S(1)}, f32[48,512]{1,0:T(8,128)S(1)}, u32[]{:S(2)}, u32[]{:S(2)}) collective-permute-start(f32[48,512]{1,0:T(8,128)S(1)} %get-tuple-element.36), channel_id=1, source_target_pairs={{0,1},{1,2},{2,3},{3,4},{4,5},{5,6},{6,7},{7,0},{8,9},{9,10},{10,1... | collective-permute-start | bytes 294920 | tf_op jit(solution)/shard_map/ppermute | solution.py:341
  66.6 4.0 %collective-permute-start.6 = (f32[48,512]{1,0:T(8,128)S(1)}, f32[48,512]{1,0:T(8,128)S(1)}, u32[]{:S(2)}, u32[]{:S(2)}) collective-permute-start(f32[48,512]{1,0:T(8,128)S(1)} %get-tuple-element.39), channel_id=1, source_target_pairs={{0,7},{1,0},{2,1},{3,2},{4,3},{5,4},{6,5},{7,6},{8,15},{9,8},{10,9... | collective-permute-start | bytes 294920 | tf_op jit(solution)/shard_map/ppermute | solution.py:342
  70.7 1.9 %collective-permute-done.2 = f32[48,512]{1,0:T(8,128)S(1)} collective-permute-done((f32[48,512]{1,0:T(8,128)S(1)}, f32[48,512]{1,0:T(8,128)S(1)}, u32[]{:S(2)}, u32[]{:S(2)}) %collective-permute-start.2) | collective-permute-done | bytes 98336 | tf_op jit(solution)/shard_map/ppermute | solution.py:341
  72.6 0.1 collective-permute-start.3
  72.7 2.7 %collective-permute-start.7 = (f32[48,512]{1,0:T(8,128)S(1)}, f32[48,512]{1,0:T(8,128)S(1)}, u32[]{:S(2)}, u32[]{:S(2)}) collective-permute-start(f32[48,512]{1,0:T(8,128)S(1)} %add.18), channel_id=1, source_target_pairs={{0,7},{1,0},{2,1},{3,2},{4,3},{5,4},{6,5},{7,6},{8,15},{9,8},{10,9... | collective-permute-start | bytes 294920 | tf_op jit(solution)/shard_map/ppermute | solution.py:342
  75.5 1.9 %collective-permute-done.3 = f32[48,512]{1,0:T(8,128)S(1)} collective-permute-done((f32[48,512]{1,0:T(8,128)S(1)}, f32[48,512]{1,0:T(8,128)S(1)}, u32[]{:S(2)}, u32[]{:S(2)}) %collective-permute-start.3) | collective-permute-done | bytes 98336 | tf_op jit(solution)/shard_map/ppermute | solution.py:341
  77.4 0.1 collective-permute-start.4
  77.5 2.7 %collective-permute-start.8 = (f32[48,512]{1,0:T(8,128)S(1)}, f32[48,512]{1,0:T(8,128)S(1)}, u32[]{:S(2)}, u32[]{:S(2)}) collective-permute-start(f32[48,512]{1,0:T(8,128)S(1)} %add.19), channel_id=1, source_target_pairs={{0,7},{1,0},{2,1},{3,2},{4,3},{5,4},{6,5},{7,6},{8,15},{9,8},{10,9... | collective-permute-start | bytes 294920 | tf_op jit(solution)/shard_map/ppermute | solution.py:342
  80.2 2.3 %collective-permute-done.4 = f32[48,512]{1,0:T(8,128)S(1)} collective-permute-done((f32[48,512]{1,0:T(8,128)S(1)}, f32[48,512]{1,0:T(8,128)S(1)}, u32[]{:S(2)}, u32[]{:S(2)}) %collective-permute-start.4) | collective-permute-done | bytes 98336 | tf_op jit(solution)/shard_map/ppermute | solution.py:341
  82.6 0.1 collective-permute-start.5
  82.7 5.4 %collective-permute-done.5.y = f32[48,512]{1,0:T(8,128)S(1)} collective-permute-done((f32[48,512]{1,0:T(8,128)S(1)}, f32[48,512]{1,0:T(8,128)S(1)}, u32[]{:S(2)}, u32[]{:S(2)}) %collective-permute-start.5) | collective-permute-done | bytes 98336 | tf_op jit(solution)/shard_map/ppermute | solution.py:341
  88.2 0.3 pack.1
  88.5 17.2 %all_to_all.10.x = f32[32,8,128]{2,1,0:T(8,128)S(1)} all-to-all(f32[32,8,128]{2,1,0:T(8,128)S(1)} %pack.1), channel_id=1, replica_groups=mesh['layer'=4,'strip'=8,'dir'=8] {'layer','strip'}, dimensions={0} | all-to-all | bytes 262144 | tf_op jit(solution)/shard_map/all_to_all | solution.py:358
  105.7 0.8 slopes.1
  (19 shorter events, 0.1 us)
Async XLA Ops:
  2.2 10.3 %collective-permute-start = (f32[32,512]{1,0:T(8,128)S(1)}, f32[32,512]{1,0:T(8,128)S(1)}, u32[]{:S(2)}, u32[]{:S(2)}) collective-permute-start(f32[32,512]{1,0:T(8,128)S(1)} %pad_maximum_fusion), channel_id=1, source_target_pairs={{0,8},{8,16},{16,24},{24,32},{32,40},{40,48},{48,56},{56,0},{1,9},... | collective-permute-start | bytes 196616 | tf_op jit(solution)/shard_map/ppermute | solution.py:233
  4.8 7.6 %collective-permute-start.1 = (f32[32,512]{1,0:T(8,128)S(1)}, f32[32,512]{1,0:T(8,128)S(1)}, u32[]{:S(2)}, u32[]{:S(2)}) collective-permute-start(f32[32,512]{1,0:T(8,128)S(1)} %pad_maximum_fusion.1), channel_id=1, source_target_pairs={{0,56},{8,0},{16,8},{24,16},{32,24},{40,32},{48,40},{56,48},{1,57}... | collective-permute-start | bytes 196616 | tf_op jit(solution)/shard_map/ppermute | solution.py:234
  6.1 1.1 %copy-start.1 = (bf16[3,1,256,512]{3,2,1,0:T(8,128)(2,1)S(1)}, bf16[3,1,256,512]{3,2,1,0:T(8,128)(2,1)}, u32[]{:S(2)}) copy-start(bf16[3,1,256,512]{3,2,1,0:T(8,128)(2,1)} %param.9) | copy-start | bytes 2359300
  7.3 1.0 copy-start.2
  8.3 0.7 copy-start.3
  14.7 7.1 %copy-start.4 = (s32[8,1,32]{2,1,0:T(1,128)S(1)}, s32[8,1,32]{2,1,0:T(1,128)}, u32[]{:S(2)}) copy-start(s32[8,1,32]{2,1,0:T(1,128)} %param.12) | copy-start | bytes 3076
  14.7 7.3 %copy-start.5 = (s32[8,1]{0,1:T(1,128)S(1)}, s32[8,1]{0,1:T(1,128)}, u32[]{:S(2)}) copy-start(s32[8,1]{0,1:T(1,128)} %param.13) | copy-start | bytes 100
  14.7 46.2 %all-to-all-start = ((f32[32,2,3,2,2,8,128]{6,5,4,3,2,1,0:T(8,128)}), f32[32,2,3,2,2,8,128]{6,5,4,3,2,1,0:T(8,128)S(1)}, u32[]{:S(2)}, u32[]{:S(2)}) async-start(f32[32,2,3,2,2,8,128]{6,5,4,3,2,1,0:T(8,128)} %get-tuple-element.31), calls=%async_computation | async-start | bytes 6291456 | tf_op jit(solution)/shard_map/all_to_all | solution.py:318
  61.0 1.2 %copy-start = (bf16[2,512,512]{2,1,0:T(8,128)(2,1)S(1)}, bf16[2,512,512]{2,1,0:T(8,128)(2,1)}, u32[]{:S(2)}) copy-start(bf16[2,512,512]{2,1,0:T(8,128)(2,1)} %table.1) | copy-start | bytes 3145732
  64.9 7.7 %collective-permute-start.2 = (f32[48,512]{1,0:T(8,128)S(1)}, f32[48,512]{1,0:T(8,128)S(1)}, u32[]{:S(2)}, u32[]{:S(2)}) collective-permute-start(f32[48,512]{1,0:T(8,128)S(1)} %get-tuple-element.36), channel_id=1, source_target_pairs={{0,1},{1,2},{2,3},{3,4},{4,5},{5,6},{6,7},{7,0},{8,9},{9,10},{10,1... | collective-permute-start | bytes 294920 | tf_op jit(solution)/shard_map/ppermute | solution.py:341
  66.6 6.1 %collective-permute-start.6 = (f32[48,512]{1,0:T(8,128)S(1)}, f32[48,512]{1,0:T(8,128)S(1)}, u32[]{:S(2)}, u32[]{:S(2)}) collective-permute-start(f32[48,512]{1,0:T(8,128)S(1)} %get-tuple-element.39), channel_id=1, source_target_pairs={{0,7},{1,0},{2,1},{3,2},{4,3},{5,4},{6,5},{7,6},{8,15},{9,8},{10,9... | collective-permute-start | bytes 294920 | tf_op jit(solution)/shard_map/ppermute | solution.py:342
  72.6 4.8 %collective-permute-start.3 = (f32[48,512]{1,0:T(8,128)S(1)}, f32[48,512]{1,0:T(8,128)S(1)}, u32[]{:S(2)}, u32[]{:S(2)}) collective-permute-start(f32[48,512]{1,0:T(8,128)S(1)} %add.15), channel_id=1, source_target_pairs={{0,1},{1,2},{2,3},{3,4},{4,5},{5,6},{6,7},{7,0},{8,9},{9,10},{10,1... | collective-permute-start | bytes 294920 | tf_op jit(solution)/shard_map/ppermute | solution.py:341
  72.7 4.7 %collective-permute-start.7 = (f32[48,512]{1,0:T(8,128)S(1)}, f32[48,512]{1,0:T(8,128)S(1)}, u32[]{:S(2)}, u32[]{:S(2)}) collective-permute-start(f32[48,512]{1,0:T(8,128)S(1)} %add.18), channel_id=1, source_target_pairs={{0,7},{1,0},{2,1},{3,2},{4,3},{5,4},{6,5},{7,6},{8,15},{9,8},{10,9... | collective-permute-start | bytes 294920 | tf_op jit(solution)/shard_map/ppermute | solution.py:342
  77.4 5.2 %collective-permute-start.4 = (f32[48,512]{1,0:T(8,128)S(1)}, f32[48,512]{1,0:T(8,128)S(1)}, u32[]{:S(2)}, u32[]{:S(2)}) collective-permute-start(f32[48,512]{1,0:T(8,128)S(1)} %add.16), channel_id=1, source_target_pairs={{0,1},{1,2},{2,3},{3,4},{4,5},{5,6},{6,7},{7,0},{8,9},{9,10},{10,1... | collective-permute-start | bytes 294920 | tf_op jit(solution)/shard_map/ppermute | solution.py:341
  77.5 5.2 %collective-permute-start.8 = (f32[48,512]{1,0:T(8,128)S(1)}, f32[48,512]{1,0:T(8,128)S(1)}, u32[]{:S(2)}, u32[]{:S(2)}) collective-permute-start(f32[48,512]{1,0:T(8,128)S(1)} %add.19), channel_id=1, source_target_pairs={{0,7},{1,0},{2,1},{3,2},{4,3},{5,4},{6,5},{7,6},{8,15},{9,8},{10,9... | collective-permute-start | bytes 294920 | tf_op jit(solution)/shard_map/ppermute | solution.py:342
  82.6 5.5 %collective-permute-start.5 = (f32[48,512]{1,0:T(8,128)S(1)}, f32[48,512]{1,0:T(8,128)S(1)}, u32[]{:S(2)}, u32[]{:S(2)}) collective-permute-start(f32[48,512]{1,0:T(8,128)S(1)} %add.17), channel_id=1, source_target_pairs={{0,1},{1,2},{2,3},{3,4},{4,5},{5,6},{6,7},{7,0},{8,9},{9,10},{10,1... | collective-permute-start | bytes 294920 | tf_op jit(solution)/shard_map/ppermute | solution.py:341
where the time goes:
time: 107 us
  blocking collectives  53.7 us (50%)
  starting transfers between devices  21.8 us (20%)
  waiting for transfers between devices  14 us (13%)
  Pallas kernels  9.58 us (9%)
  local copies, waits for them, and re-layouts  5.2 us (5%)
  between operations  1.44 us (1%)
    all_gather x1, blocking collectives, shards(): places = lax.all_gather(places, 'layer').reshape(LAYERS * 2 * NDIR)  36.4 us
    all_to_all x1, blocking collectives, shards(): rows = lax.all_to_all(packed, PLANE, 0, 0, tiled=True)  17.2 us
    ppermute x4, waiting for transfers between devices, shards(): up = lambda x: lax.ppermute(x, 'dir', neighbours(count, 1))  11.6 us
    ppermute x3, starting transfers between devices, shards(): down = lambda x: lax.ppermute(x, 'dir', neighbours(count, -1))  9.49 us
    all_to_all x1, starting transfers between devices, shards(): gathered = lax.all_to_all(images, PLANE, 0, 0, tiled=True)  7.07 us
    unnamed x12, local copies, waits for them, and re-layouts  4.11 us
    pallas_call x1, Pallas kernels, shards(): pl.pallas_call(inner_kernel, in_specs=[SCALARS, whole(ROWS, COLS), whole(...  3.42 us
    pallas_call x1, Pallas kernels, shards(): pl.pallas_call(pupil_kernel, in_specs=[SCALARS, SCALARS, whole(CHUNKS * 2...  2.71 us
  transfers between devices with their start and end apart: 10, of which 5 were waited for; matrix products, arithmetic and copies ran while one was open for 0% of the time, Pallas kernels for 3%

commit v1 on v0

--- a/solution.py
+++ b/solution.py
@@ -31,12 +31,22 @@
     return total
 
 
+def ends_kernel(screen, fresh, coef, begin, last, screen_on, fresh_on, coef_on):
+    begin[0:16, :] = screen[0:16, :]
+    last[0:16, :] = screen[ROWS - 16 : ROWS, :]
+    for t in range(2):
+        at = slice(16 + 8 * t, 24 + 8 * t)
+        begin[at, :] = fresh[t, 0:16, :].astype(jnp.float32)[0:8, :]
+        last[at, :] = fresh[t, ROWS - 16 : ROWS, :].astype(jnp.float32)[8:16, :]
+    screen_on[...] = screen[...]
+    fresh_on[...] = fresh[...]
+    coef_on[...] = coef[...]
+
+
 def inner_kernel(
-    wind, screen, fresh, coef, column_table, flats, near0, fresh0, near1, near2, near3, table, taps, s3, s1, s2
+    wind, screen, fresh, coef, flats, near0, fresh0, near1, near2, near3, s3, s1, s2
 ):
     shift = wind[0] + 2
-    table[...] = column_table[...]
-    taps[...] = coef[...]
     near0[0] = screen[0:16, :]
     near0[1] = screen[ROWS - 16 : ROWS, :]
     fresh0[0] = fresh[:, 0:32, :]
@@ -126,8 +136,7 @@
         copy.wait()
 
 
-def pupil_kernel(mine, places, x, table, *refs):
-    *outs, feet, pupils = refs
+def feet_kernel(places, x, feet):
     feet[...] = jnp.zeros(feet.shape, jnp.float32)
     lane = lax.broadcasted_iota(jnp.int32, (GROUP, LANES), 1)
 
@@ -147,6 +156,9 @@
                 at = (m, pl.ds(d * GROUP, GROUP), pl.ds(i * LANES, LANES))
                 feet[at] = feet[at] + piece
 
+
+def pupil_kernel(mine, feet, table, *refs):
+    *outs, pupils = refs
     total = None
     for m in range(NM):
         whole = feet[m]
@@ -162,8 +174,11 @@
         out[...] = pupils[(mine[0] + j) % NDIR]
 
 
-def pack_kernel(x, y, z, out):
-    total = x[...] + y[...] + z[...]
+def pack_kernel(*refs):
+    *terms, out = refs
+    total = terms[0][...]
+    for term in terms[1:]:
+        total = total + term[...]
     tiles = [total[8 * j : 8 * j + 8] for j in range(6)]
 
     lane = lax.broadcasted_iota(jnp.int32, (8, LANES), 1)
@@ -225,15 +240,33 @@
 def shards(screen, innovation, coef, wind, row_blocks, table_index, row_table, column_table):
     state = screen[0]
     fresh = innovation[:, 0]
-    taps = jnp.swapaxes(coef, 0, 1)
     strips = lax.axis_size("strip")
 
-    last = [state[-16:], fresh[0, -8:].astype(jnp.float32), fresh[1, -8:].astype(jnp.float32)]
-    begin = [state[:16], fresh[0, :8].astype(jnp.float32), fresh[1, :8].astype(jnp.float32)]
-    low = lax.ppermute(jnp.concatenate(last, axis=0), "strip", neighbours(strips, 1))
-    high = lax.ppermute(jnp.concatenate(begin, axis=0), "strip", neighbours(strips, -1))
-
     near = jax.ShapeDtypeStruct((32, COLS), jnp.float32)
+    taps = jax.ShapeDtypeStruct((TAPS, 1, COLS), jnp.float32)
+    begin, last, state, fresh, taps = pl.pallas_call(
+        ends_kernel,
+        in_specs=[whole(ROWS, COLS), whole(STEPS, ROWS, COLS), whole(TAPS, 1, COLS)],
+        out_specs=[
+            whole(32, COLS),
+            whole(32, COLS),
+            whole(ROWS, COLS),
+            whole(STEPS, ROWS, COLS),
+            whole(TAPS, 1, COLS),
+        ],
+        out_shape=[
+            near,
+            near,
+            jax.ShapeDtypeStruct((ROWS, COLS), jnp.float32),
+            jax.ShapeDtypeStruct((STEPS, ROWS, COLS), jnp.bfloat16),
+            taps,
+        ],
+        compiler_params=room(24),
+        name="ends",
+    )(state, fresh, jnp.swapaxes(coef, 0, 1))
+    low = lax.ppermute(last, "strip", neighbours(strips, 1))
+    high = lax.ppermute(begin, "strip", neighbours(strips, -1))
+
     *inside, unfinished = pl.pallas_call(
         inner_kernel,
         in_specs=[
@@ -241,7 +274,6 @@
             whole(ROWS, COLS),
             whole(STEPS, ROWS, COLS),
             whole(TAPS, 1, COLS),
-            whole(NM, PC, COLS),
         ],
         out_specs=[
             whole(STEPS, ROWS, COLS),
@@ -250,8 +282,6 @@
             whole(32, COLS),
             whole(32, COLS),
             whole(16, COLS),
-            whole(NM, PC, COLS),
-            whole(TAPS, 1, COLS),
             whole(ROWS, COLS),
         ],
         out_shape=[
@@ -261,17 +291,15 @@
             near,
             near,
             jax.ShapeDtypeStruct((16, COLS), jnp.float32),
-            jax.ShapeDtypeStruct((NM, PC, COLS), jnp.bfloat16),
-            jax.ShapeDtypeStruct((TAPS, 1, COLS), jnp.float32),
             jax.ShapeDtypeStruct((ROWS, COLS), jnp.float32),
         ],
         scratch_shapes=[pltpu.VMEM((ROWS, COLS), jnp.float32)] * 2,
-        compiler_params=room(50),
+        compiler_params=room(24),
         cost_estimate=pl.CostEstimate(
-            flops=12 * STEPS * ROWS * COLS, bytes_accessed=14 * ROWS * COLS, transcendentals=0
+            flops=12 * STEPS * ROWS * COLS, bytes_accessed=100 * ROWS * COLS, transcendentals=0
         ),
         name="inner",
-    )(wind, state, fresh, taps, column_table)
+    )(wind, state, fresh, taps)
 
     anywhere = pl.BlockSpec(memory_space=pl.ANY)
     images, screen_out = pl.pallas_call(
@@ -309,8 +337,9 @@
         *inside[1:3],
         low,
         high,
-        inside[7],
-        *inside[3:7],
+        taps,
+        *inside[3:6],
+        column_table,
         inside[0],
         unfinished,
     )
@@ -319,42 +348,37 @@
     places = jnp.stack([row_blocks[:, 0, 0], table_index[:, 0]])
     places = lax.all_gather(places, "layer").reshape(LAYERS * 2 * NDIR)
     mine = lax.axis_index("dir").astype(jnp.int32).reshape(1)
+    feet = pl.pallas_call(
+        feet_kernel,
+        in_specs=[SCALARS, whole(CHUNKS * 2, STEPS, NM, 2, 8, LANES)],
+        out_specs=whole(NM, NDIR * GROUP, PR),
+        out_shape=jax.ShapeDtypeStruct((NM, NDIR * GROUP, PR), jnp.float32),
+        compiler_params=room(24),
+        cost_estimate=pl.CostEstimate(flops=0, bytes_accessed=100 * ROWS * COLS, transcendentals=0),
+        name="feet",
+    )(places, gathered.reshape(CHUNKS * 2, STEPS, NM, 2, 8, LANES))
     pupils = pl.pallas_call(
         pupil_kernel,
-        in_specs=[
-            SCALARS,
-            SCALARS,
-            whole(CHUNKS * 2, STEPS, NM, 2, 8, LANES),
-            whole(NM, PR, PR),
-        ],
+        in_specs=[SCALARS, whole(NM, NDIR * GROUP, PR), whole(NM, PR, PR)],
         out_specs=[whole(GROUP, PR)] * NDIR,
         out_shape=[jax.ShapeDtypeStruct((GROUP, PR), jnp.float32)] * NDIR,
-        scratch_shapes=[
-            pltpu.VMEM((NM, NDIR * GROUP, PR), jnp.float32),
-            pltpu.VMEM((NDIR, GROUP, PR), jnp.float32),
-        ],
+        scratch_shapes=[pltpu.VMEM((NDIR, GROUP, PR), jnp.float32)],
         compiler_params=room(24),
         name="pupil",
-    )(mine, places, gathered.reshape(CHUNKS * 2, STEPS, NM, 2, 8, LANES), row_table)
+    )(mine, feet, row_table)
 
     count = lax.axis_size("dir")
-    up = lambda x: lax.ppermute(x, "dir", neighbours(count, 1))
-    down = lambda x: lax.ppermute(x, "dir", neighbours(count, -1))
-    rising = up(pupils[4])
-    falling = down(pupils[5])
-    rising = up(pupils[3] + rising)
-    falling = down(pupils[6] + falling)
-    rising = up(pupils[2] + rising)
-    falling = down(pupils[7] + falling)
-    rising = up(pupils[1] + rising)
+    terms = [pupils[0]] + [
+        lax.ppermute(pupils[j], "dir", neighbours(count, j)) for j in (4, 3, 5, 2, 6, 1, 7)
+    ]
     packed = pl.pallas_call(
         pack_kernel,
-        in_specs=[whole(GROUP, PR)] * 3,
+        in_specs=[whole(GROUP, PR)] * NDIR,
         out_specs=whole(CHUNKS, 8, LANES),
         out_shape=jax.ShapeDtypeStruct((CHUNKS, 8, LANES), jnp.float32),
         compiler_params=room(16),
         name="pack",
-    )(pupils[0], rising, falling)
+    )(*terms)
     rows = lax.all_to_all(packed, PLANE, 0, 0, tiled=True)
     slopes = pl.pallas_call(
         slope_kernel,

time: 107 us -> 102 us (0.953)
  blocking collectives: 53.7 us -> 49.1 us
  starting transfers between devices: 21.8 us -> 26.2 us
  local copies, waits for them, and re-layouts: 5.2 us -> 3.29 us
  Pallas kernels: 9.58 us -> 8.44 us
  waiting for transfers between devices: 14 us -> 12.9 us
    all_to_all x1, blocking collectives: 17.2 us -> 12.7 us  [shards(): rows = lax.all_to_all(packed, PLANE, 0, 0, tiled=True)]
    ppermute x9, starting transfers between devices: 14.7 us -> 19.1 us  [the longest x7 15.8 us: shards(): lax.ppermute(pupils[j], 'dir', neighbours(count, j))]
    pallas_call x1, Pallas kernels: 3.42 us -> 2.14 us  [shards(): pl.pallas_call(inner_kernel, in_specs=[SCALARS, whole(ROWS, COLS), whole(...]
    unnamed x12 -> x14, local copies, waits for them, and re-layouts: 4.11 us -> 2.98 us
    ppermute x9, waiting for transfers between devices: 11.6 us -> 10.6 us  [the longest x7 10.3 us: shards(): lax.ppermute(pupils[j], 'dir', neighbours(count, j))]
    pallas_call x2 -> x4, Pallas kernels: 3.02 us -> 3.15 us  [the longest x1 1.67 us: shards(): pl.pallas_call(feet_kernel, in_specs=[SCALARS, whole(CHUNKS * 2, STEPS, N...]
  transfers between devices with their start and end apart: 10 -> 10, of which waited for: 5 -> 6; matrix products, arithmetic and copies ran while one was open for 0% -> 0% of each run, Pallas kernels for 3% -> 2%
where the time goes in v1:
time: 102 us; the launch traced here: 101 us
  blocking collectives  49.1 us (48%)
  starting transfers between devices  26.2 us (26%)
  waiting for transfers between devices  12.9 us (13%)
  Pallas kernels  8.44 us (8%)
  local copies, waits for them, and re-layouts  3.29 us (3%)
  between operations  1.4 us (1%)
    all_gather x1, blocking collectives, shards(): places = lax.all_gather(places, 'layer').reshape(LAYERS * 2 * NDIR)  36.4 us
    ppermute x7, starting transfers between devices, shards(): lax.ppermute(pupils[j], 'dir', neighbours(count, j))  15.8 us
    all_to_all x1, blocking collectives, shards(): rows = lax.all_to_all(packed, PLANE, 0, 0, tiled=True)  12.7 us
    ppermute x7, waiting for transfers between devices, shards(): lax.ppermute(pupils[j], 'dir', neighbours(count, j))  10.3 us
    all_to_all x1, starting transfers between devices, shards(): gathered = lax.all_to_all(images, PLANE, 0, 0, tiled=True)  7.14 us
    unnamed x14, local copies, waits for them, and re-layouts  2.98 us
    ppermute x1, starting transfers between devices, shards(): low = lax.ppermute(last, 'strip', neighbours(strips, 1))  2.61 us
    all_to_all x1, waiting for transfers between devices, shards(): gathered = lax.all_to_all(images, PLANE, 0, 0, tiled=True)  2.38 us
  transfers between devices with their start and end apart: 10, of which 6 were waited for; matrix products, arithmetic and copies ran while one was open for 0% of the time, Pallas kernels for 2%

profile of v1, /device:TPU:1, one launch (start us, length us, event | category | flops | bytes accessed | tf_op | source)
XLA Modules:
  0.0 101.4 jit_solution(1940070914103544251)
XLA Ops:
  0.7 1.2 %copy-done.2 = bf16[3,1,256,512]{3,2,1,0:T(8,128)(2,1)S(1)} copy-done((bf16[3,1,256,512]{3,2,1,0:T(8,128)(2,1)S(1)}, bf16[3,1,256,512]{3,2,1,0:T(8,128)(2,1)}, u32[]{:S(2)}) %copy-start.2) | copy-done | bytes 786456
  1.9 1.0 %copy-done.3 = f32[1,256,512]{2,1,0:T(8,128)S(1)} copy-done((f32[1,256,512]{2,1,0:T(8,128)S(1)}, f32[1,256,512]{2,1,0:T(8,128)}, u32[]{:S(2)}) %copy-start.3) | copy-done | bytes 524312
  2.9 0.7 copy-done.4
  3.6 0.1 ends.1
  3.7 2.6 %collective-permute-start = (f32[32,512]{1,0:T(8,128)S(1)}, f32[32,512]{1,0:T(8,128)S(1)}, u32[]{:S(2)}, u32[]{:S(2)}) collective-permute-start(f32[32,512]{1,0:T(8,128)S(1)} %get-tuple-element.29), channel_id=1, source_target_pairs={{0,8},{8,16},{16,24},{24,32},{32,40},{40,48},{48,56},{56,0},{1,9},... | collective-permute-start | bytes 196616 | tf_op jit(solution)/shard_map/ppermute | solution.py:267
  6.3 0.7 collective-permute-start.1
  7.6 2.1 %inner.1 = (bf16[3,256,512]{2,1,0:T(8,128)(2,1)S(1)}, f32[2,16,512]{2,1,0:T(8,128)S(1)}, bf16[2,3,32,512]{3,2,1,0:T(8,128)(2,1)S(1)}, f32[32,512]{1,0:T(8,128)S(...) custom-call(s32[1]{0:T(128)S(6)} %copy.12.wind, f32[256,512]{1,0:T(8,128)S(1)} %get-tuple-element.24.screen, ...), custom_call_target="tpu_custom_call" | custom-call | flops 4718592 | bytes 13107200 | tf_op jit(solution)/shard_map/inner/pallas_call | solution.py:270
  9.8 0.0 collective-permute-done.low
  9.8 0.2 collective-permute-done.1.high
  10.0 2.3 %outer.1 = (f32[32,2,3,2,2,8,128]{6,5,4,3,2,1,0:T(8,128)}, f32[256,512]{1,0:T(8,128)}) custom-call(s32[1]{0:T(128)S(6)} %copy.12.wind, f32[2,16,512]{2,1,0:T(8,128)S(1)} %get-tuple-element.27.near0, bf16[2,3,32,512]{3,2,1,0:T(8,128)(2,1)S(1)} %get-tuple-element.28.fresh0, f32[32,512]{1,0:T(8,128)S(1)} %collective-permute-done.low, ...), custom_call_target="tpu_custom_call", output_to_operand_aliasing={{1}: (11, {})} | custom-call | tf_op jit(solution)/shard_map/outer/pallas_call | solution.py:305
  12.3 0.0 copy-start.5
  12.3 0.0 copy-start.6
  12.3 7.1 %all-to-all-start = ((f32[32,2,3,2,2,8,128]{6,5,4,3,2,1,0:T(8,128)}), f32[32,2,3,2,2,8,128]{6,5,4,3,2,1,0:T(8,128)S(1)}, u32[]{:S(2)}, u32[]{:S(2)}) async-start(f32[32,2,3,2,2,8,128]{6,5,4,3,2,1,0:T(8,128)} %get-tuple-element.37), calls=%async_computation | async-start | bytes 6291456 | tf_op jit(solution)/shard_map/all_to_all | solution.py:347
  19.5 0.2 slice_reduce_fusion
  19.8 36.4 %all-gather.1 = s32[4,2,8]{2,1,0:T(2,128)S(1)} all-gather(s32[1,2,8]{2,1,0:T(2,128)S(1)} %add_bitcast_fusion), channel_id=2, replica_groups=mesh['layer'=4,'strip'=8,'dir'=8] {'layer'}, dimensions={0}, use_global_device_ids=true | all-gather | bytes 320 | tf_op jit(solution)/shard_map/all_gather | solution.py:349
  56.2 0.1 reshape.14.places
  56.3 2.4 %all-to-all-done = f32[32,2,3,2,2,8,128]{6,5,4,3,2,1,0:T(8,128)S(1)} async-done(((f32[32,2,3,2,2,8,128]{6,5,4,3,2,1,0:T(8,128)}), f32[32,2,3,2,2,8,128]{6,5,4,3,2,1,0:T(8,128)S(1)}, u32[]{:S(2)}, u32[]{:S(2)}) %all-to-all-start) | async-done | bytes 3145760 | tf_op jit(solution)/shard_map/all_to_all | solution.py:347
  58.7 1.7 %feet.1 = f32[2,384,512]{2,1,0:T(8,128)S(1)} custom-call(s32[64]{0:T(128)S(1)} %reshape.14.places, f32[64,3,2,2,8,128]{5,4,3,2,1,0:T(8,128)S(1)} %bitcast.10), custom_call_target="tpu_custom_call" | custom-call | bytes 13107200 | tf_op jit(solution)/shard_map/feet/pallas_call | solution.py:351
  60.3 1.1 %pupil.1 = (f32[48,512]{1,0:T(8,128)S(1)}, f32[48,512]{1,0:T(8,128)S(1)}, f32[48,512]{1,0:T(8,128)S(1)}, f32[48,512]{1,0:T(8,128)S(1)}, f32[48,512]{1,0:T(8,128)...) custom-call(s32[1]{0:T(128)} %bitcast.4.mine, f32[2,384,512]{2,1,0:T(8,128)S(1)} %feet.1, ...), custom_call_target="tpu_custom_call" | custom-call | tf_op jit(solution)/shard_map/pupil/pallas_call | solution.py:360
  61.4 7.0 %collective-permute-start.2 = (f32[48,512]{1,0:T(8,128)S(1)}, f32[48,512]{1,0:T(8,128)S(1)}, u32[]{:S(2)}, u32[]{:S(2)}) collective-permute-start(f32[48,512]{1,0:T(8,128)S(1)} %get-tuple-element.39), channel_id=1, source_target_pairs={{0,4},{1,5},{2,6},{3,7},{4,0},{5,1},{6,2},{7,3},{8,12},{9,13},{10,... | collective-permute-start | bytes 294920 | tf_op jit(solution)/shard_map/ppermute | solution.py:372
  68.4 1.7 %collective-permute-start.3 = (f32[48,512]{1,0:T(8,128)S(1)}, f32[48,512]{1,0:T(8,128)S(1)}, u32[]{:S(2)}, u32[]{:S(2)}) collective-permute-start(f32[48,512]{1,0:T(8,128)S(1)} %get-tuple-element.40), channel_id=1, source_target_pairs={{0,3},{1,4},{2,5},{3,6},{4,7},{5,0},{6,1},{7,2},{8,11},{9,12},{10,... | collective-permute-start | bytes 294920 | tf_op jit(solution)/shard_map/ppermute | solution.py:372
  70.1 2.8 %collective-permute-start.4 = (f32[48,512]{1,0:T(8,128)S(1)}, f32[48,512]{1,0:T(8,128)S(1)}, u32[]{:S(2)}, u32[]{:S(2)}) collective-permute-start(f32[48,512]{1,0:T(8,128)S(1)} %get-tuple-element.41), channel_id=1, source_target_pairs={{0,5},{1,6},{2,7},{3,0},{4,1},{5,2},{6,3},{7,4},{8,13},{9,14},{10,... | collective-permute-start | bytes 294920 | tf_op jit(solution)/shard_map/ppermute | solution.py:372
  72.9 1.2 %collective-permute-start.5 = (f32[48,512]{1,0:T(8,128)S(1)}, f32[48,512]{1,0:T(8,128)S(1)}, u32[]{:S(2)}, u32[]{:S(2)}) collective-permute-start(f32[48,512]{1,0:T(8,128)S(1)} %get-tuple-element.42), channel_id=1, source_target_pairs={{0,2},{1,3},{2,4},{3,5},{4,6},{5,7},{6,0},{7,1},{8,10},{9,11},{10,... | collective-permute-start | bytes 294920 | tf_op jit(solution)/shard_map/ppermute | solution.py:372
  74.1 2.4 %collective-permute-start.6 = (f32[48,512]{1,0:T(8,128)S(1)}, f32[48,512]{1,0:T(8,128)S(1)}, u32[]{:S(2)}, u32[]{:S(2)}) collective-permute-start(f32[48,512]{1,0:T(8,128)S(1)} %get-tuple-element.43), channel_id=1, source_target_pairs={{0,6},{1,7},{2,0},{3,1},{4,2},{5,3},{6,4},{7,5},{8,14},{9,15},{10,... | collective-permute-start | bytes 294920 | tf_op jit(solution)/shard_map/ppermute | solution.py:372
  76.5 0.8 collective-permute-start.7
  77.2 5.2 %collective-permute-done.3.refs_2_ = f32[48,512]{1,0:T(8,128)S(1)} collective-permute-done((f32[48,512]{1,0:T(8,128)S(1)}, f32[48,512]{1,0:T(8,128)S(1)}, u32[]{:S(2)}, u32[]{:S(2)}) %collective-permute-start.3) | collective-permute-done | bytes 98336 | tf_op jit(solution)/shard_map/ppermute | solution.py:372
  82.4 1.5 %collective-permute-done.6.refs_5_ = f32[48,512]{1,0:T(8,128)S(1)} collective-permute-done((f32[48,512]{1,0:T(8,128)S(1)}, f32[48,512]{1,0:T(8,128)S(1)}, u32[]{:S(2)}, u32[]{:S(2)}) %collective-permute-start.6) | collective-permute-done | bytes 98336 | tf_op jit(solution)/shard_map/ppermute | solution.py:372
  83.9 2.7 %collective-permute-done.7.refs_6_ = f32[48,512]{1,0:T(8,128)S(1)} collective-permute-done((f32[48,512]{1,0:T(8,128)S(1)}, f32[48,512]{1,0:T(8,128)S(1)}, u32[]{:S(2)}, u32[]{:S(2)}) %collective-permute-start.7) | collective-permute-done | bytes 98336 | tf_op jit(solution)/shard_map/ppermute | solution.py:372
  86.6 0.9 collective-permute-done.8.refs_7_
  87.5 0.3 pack.1
  87.9 12.7 %all_to_all.10.x = f32[32,8,128]{2,1,0:T(8,128)S(1)} all-to-all(f32[32,8,128]{2,1,0:T(8,128)S(1)} %pack.1), channel_id=1, replica_groups=mesh['layer'=4,'strip'=8,'dir'=8] {'layer','strip'}, dimensions={0} | all-to-all | bytes 262144 | tf_op jit(solution)/shard_map/all_to_all | solution.py:382
  100.6 0.8 slopes.1
  (14 shorter events, 0.0 us)
Async XLA Ops:
  0.6 9.4 %copy-start.1 = (bf16[2,512,512]{2,1,0:T(8,128)(2,1)S(1)}, bf16[2,512,512]{2,1,0:T(8,128)(2,1)}, u32[]{:S(2)}) copy-start(bf16[2,512,512]{2,1,0:T(8,128)(2,1)} %table.2) | copy-start | bytes 3145732
  0.6 1.2 %copy-start.2 = (bf16[3,1,256,512]{3,2,1,0:T(8,128)(2,1)S(1)}, bf16[3,1,256,512]{3,2,1,0:T(8,128)(2,1)}, u32[]{:S(2)}) copy-start(bf16[3,1,256,512]{3,2,1,0:T(8,128)(2,1)} %param.9) | copy-start | bytes 2359300
  1.9 1.0 %copy-start.3 = (f32[1,256,512]{2,1,0:T(8,128)S(1)}, f32[1,256,512]{2,1,0:T(8,128)}, u32[]{:S(2)}) copy-start(f32[1,256,512]{2,1,0:T(8,128)} %param.8) | copy-start | bytes 1572868
  2.9 0.7 copy-start.4
  3.7 6.1 %collective-permute-start = (f32[32,512]{1,0:T(8,128)S(1)}, f32[32,512]{1,0:T(8,128)S(1)}, u32[]{:S(2)}, u32[]{:S(2)}) collective-permute-start(f32[32,512]{1,0:T(8,128)S(1)} %get-tuple-element.29), channel_id=1, source_target_pairs={{0,8},{8,16},{16,24},{24,32},{32,40},{40,48},{48,56},{56,0},{1,9},... | collective-permute-start | bytes 196616 | tf_op jit(solution)/shard_map/ppermute | solution.py:267
  6.3 3.7 %collective-permute-start.1 = (f32[32,512]{1,0:T(8,128)S(1)}, f32[32,512]{1,0:T(8,128)S(1)}, u32[]{:S(2)}, u32[]{:S(2)}) collective-permute-start(f32[32,512]{1,0:T(8,128)S(1)} %get-tuple-element.30), channel_id=1, source_target_pairs={{0,56},{8,0},{16,8},{24,16},{32,24},{40,32},{48,40},{56,48},{1,57}... | collective-permute-start | bytes 196616 | tf_op jit(solution)/shard_map/ppermute | solution.py:268
  12.3 7.2 %copy-start.5 = (s32[8,1,32]{2,1,0:T(1,128)S(1)}, s32[8,1,32]{2,1,0:T(1,128)}, u32[]{:S(2)}) copy-start(s32[8,1,32]{2,1,0:T(1,128)} %param.12) | copy-start | bytes 3076
  12.3 7.4 %copy-start.6 = (s32[8,1]{0,1:T(1,128)S(1)}, s32[8,1]{0,1:T(1,128)}, u32[]{:S(2)}) copy-start(s32[8,1]{0,1:T(1,128)} %param.13) | copy-start | bytes 100
  12.3 46.3 %all-to-all-start = ((f32[32,2,3,2,2,8,128]{6,5,4,3,2,1,0:T(8,128)}), f32[32,2,3,2,2,8,128]{6,5,4,3,2,1,0:T(8,128)S(1)}, u32[]{:S(2)}, u32[]{:S(2)}) async-start(f32[32,2,3,2,2,8,128]{6,5,4,3,2,1,0:T(8,128)} %get-tuple-element.37), calls=%async_computation | async-start | bytes 6291456 | tf_op jit(solution)/shard_map/all_to_all | solution.py:347
  58.7 1.7 %copy-start = (bf16[2,512,512]{2,1,0:T(8,128)(2,1)S(1)}, bf16[2,512,512]{2,1,0:T(8,128)(2,1)}, u32[]{:S(2)}) copy-start(bf16[2,512,512]{2,1,0:T(8,128)(2,1)} %table.3) | copy-start | bytes 3145732
  61.4 15.0 %collective-permute-start.2 = (f32[48,512]{1,0:T(8,128)S(1)}, f32[48,512]{1,0:T(8,128)S(1)}, u32[]{:S(2)}, u32[]{:S(2)}) collective-permute-start(f32[48,512]{1,0:T(8,128)S(1)} %get-tuple-element.39), channel_id=1, source_target_pairs={{0,4},{1,5},{2,6},{3,7},{4,0},{5,1},{6,2},{7,3},{8,12},{9,13},{10,... | collective-permute-start | bytes 294920 | tf_op jit(solution)/shard_map/ppermute | solution.py:372
  68.4 14.0 %collective-permute-start.3 = (f32[48,512]{1,0:T(8,128)S(1)}, f32[48,512]{1,0:T(8,128)S(1)}, u32[]{:S(2)}, u32[]{:S(2)}) collective-permute-start(f32[48,512]{1,0:T(8,128)S(1)} %get-tuple-element.40), channel_id=1, source_target_pairs={{0,3},{1,4},{2,5},{3,6},{4,7},{5,0},{6,1},{7,2},{8,11},{9,12},{10,... | collective-permute-start | bytes 294920 | tf_op jit(solution)/shard_map/ppermute | solution.py:372
  70.1 12.3 %collective-permute-start.4 = (f32[48,512]{1,0:T(8,128)S(1)}, f32[48,512]{1,0:T(8,128)S(1)}, u32[]{:S(2)}, u32[]{:S(2)}) collective-permute-start(f32[48,512]{1,0:T(8,128)S(1)} %get-tuple-element.41), channel_id=1, source_target_pairs={{0,5},{1,6},{2,7},{3,0},{4,1},{5,2},{6,3},{7,4},{8,13},{9,14},{10,... | collective-permute-start | bytes 294920 | tf_op jit(solution)/shard_map/ppermute | solution.py:372
  72.9 9.5 %collective-permute-start.5 = (f32[48,512]{1,0:T(8,128)S(1)}, f32[48,512]{1,0:T(8,128)S(1)}, u32[]{:S(2)}, u32[]{:S(2)}) collective-permute-start(f32[48,512]{1,0:T(8,128)S(1)} %get-tuple-element.42), channel_id=1, source_target_pairs={{0,2},{1,3},{2,4},{3,5},{4,6},{5,7},{6,0},{7,1},{8,10},{9,11},{10,... | collective-permute-start | bytes 294920 | tf_op jit(solution)/shard_map/ppermute | solution.py:372
  74.1 9.8 %collective-permute-start.6 = (f32[48,512]{1,0:T(8,128)S(1)}, f32[48,512]{1,0:T(8,128)S(1)}, u32[]{:S(2)}, u32[]{:S(2)}) collective-permute-start(f32[48,512]{1,0:T(8,128)S(1)} %get-tuple-element.43), channel_id=1, source_target_pairs={{0,6},{1,7},{2,0},{3,1},{4,2},{5,3},{6,4},{7,5},{8,14},{9,15},{10,... | collective-permute-start | bytes 294920 | tf_op jit(solution)/shard_map/ppermute | solution.py:372
  76.5 10.2 %collective-permute-start.7 = (f32[48,512]{1,0:T(8,128)S(1)}, f32[48,512]{1,0:T(8,128)S(1)}, u32[]{:S(2)}, u32[]{:S(2)}) collective-permute-start(f32[48,512]{1,0:T(8,128)S(1)} %get-tuple-element.44), channel_id=1, source_target_pairs={{0,1},{1,2},{2,3},{3,4},{4,5},{5,6},{6,7},{7,0},{8,9},{9,10},{10,1... | collective-permute-start | bytes 294920 | tf_op jit(solution)/shard_map/ppermute | solution.py:372
  82.4 5.1 %collective-permute-start.8 = (f32[48,512]{1,0:T(8,128)S(1)}, f32[48,512]{1,0:T(8,128)S(1)}, u32[]{:S(2)}, u32[]{:S(2)}) collective-permute-start(f32[48,512]{1,0:T(8,128)S(1)} %get-tuple-element.45), channel_id=1, source_target_pairs={{0,7},{1,0},{2,1},{3,2},{4,3},{5,4},{6,5},{7,6},{8,15},{9,8},{10,9... | collective-permute-start | bytes 294920 | tf_op jit(solution)/shard_map/ppermute | solution.py:372

commit v2 on v1

--- a/solution.py
+++ b/solution.py
@@ -20,6 +20,7 @@
 LANES = 128
 GROUP = STEPS * 2 * 8
 PLANE = ("layer", "strip")
+PARTS = ((0,), (1,), (2,), (3,), (4,), (5,), (6,), (7,))
 
 
 def advance(window, fresh, coef, shift):
@@ -170,15 +171,13 @@
             )
             total = product if total is None else total + product
     pupils[...] = total.reshape(pupils.shape)
-    for j, out in enumerate(outs):
-        out[...] = pupils[(mine[0] + j) % NDIR]
-
-
-def pack_kernel(*refs):
-    *terms, out = refs
-    total = terms[0][...]
-    for term in terms[1:]:
-        total = total + term[...]
+    for out, parts in zip(outs, PARTS):
+        for at, j in enumerate(parts):
+            out[at * GROUP : at * GROUP + GROUP, :] = pupils[(mine[0] + j) % NDIR]
+
+
+def pack_kernel(here, up1, down1, up2, down2, up3, out):
+    total = here[...] + up1[...] + down1[...] + up2[...] + down2[...] + up3[...]
     tiles = [total[8 * j : 8 * j + 8] for j in range(6)]
 
     lane = lax.broadcasted_iota(jnp.int32, (8, LANES), 1)
@@ -360,20 +359,27 @@
     pupils = pl.pallas_call(
         pupil_kernel,
         in_specs=[SCALARS, whole(NM, NDIR * GROUP, PR), whole(NM, PR, PR)],
-        out_specs=[whole(GROUP, PR)] * NDIR,
-        out_shape=[jax.ShapeDtypeStruct((GROUP, PR), jnp.float32)] * NDIR,
+        out_specs=[whole(len(parts) * GROUP, PR) for parts in PARTS],
+        out_shape=[jax.ShapeDtypeStruct((len(parts) * GROUP, PR), jnp.float32) for parts in PARTS],
         scratch_shapes=[pltpu.VMEM((NDIR, GROUP, PR), jnp.float32)],
         compiler_params=room(24),
         name="pupil",
     )(mine, feet, row_table)
 
     count = lax.axis_size("dir")
-    terms = [pupils[0]] + [
-        lax.ppermute(pupils[j], "dir", neighbours(count, j)) for j in (4, 3, 5, 2, 6, 1, 7)
-    ]
+    send = lambda x, by: lax.ppermute(x, "dir", neighbours(count, by))
+    far = send(pupils[4], -2)
+    up3 = send(pupils[3], 3)
+    down3 = send(pupils[5], -1)
+    up2 = send(pupils[2], 2)
+    down1 = send(pupils[7], -1)
+    up1 = send(pupils[1], 1)
+    down2 = send(pupils[6] + down3 + far, -2)
+    terms = [pupils[0], up1, down1, up2, down2, up3]
+
     packed = pl.pallas_call(
         pack_kernel,
-        in_specs=[whole(GROUP, PR)] * NDIR,
+        in_specs=[whole(GROUP, PR)] * 6,
         out_specs=whole(CHUNKS, 8, LANES),
         out_shape=jax.ShapeDtypeStruct((CHUNKS, 8, LANES), jnp.float32),
         compiler_params=room(16),

time: 102 us -> 98.4 us (0.965)
  waiting for transfers between devices: 12.9 us -> 9.45 us
  blocking collectives: 49.1 us -> 52.1 us
  starting transfers between devices: 26.2 us -> 23.4 us
    ppermute x7, waiting for transfers between devices: 10.3 us -> 6.83 us  [shards(): send = lambda x, by: lax.ppermute(x, 'dir', neighbours(count, by))]
    all_to_all x1, blocking collectives: 12.7 us -> 15.7 us  [shards(): rows = lax.all_to_all(packed, PLANE, 0, 0, tiled=True)]
    ppermute x7, starting transfers between devices: 15.8 us -> 13 us  [shards(): send = lambda x, by: lax.ppermute(x, 'dir', neighbours(count, by))]
  transfers between devices with their start and end apart: 10 -> 10, of which waited for: 6 -> 4; matrix products, arithmetic and copies ran while one was open for 0% -> 0% of each run, Pallas kernels for 2% -> 2%
where the time goes in v2:
time: 98.4 us; the launch traced here: 98.1 us
  blocking collectives  52.1 us (53%)
  starting transfers between devices  23.4 us (24%)
  waiting for transfers between devices  9.45 us (10%)
  Pallas kernels  8.44 us (9%)
  local copies, waits for them, and re-layouts  3.29 us (3%)
  between operations  1.4 us (1%)
    all_gather x1, blocking collectives, shards(): places = lax.all_gather(places, 'layer').reshape(LAYERS * 2 * NDIR)  36.4 us
    all_to_all x1, blocking collectives, shards(): rows = lax.all_to_all(packed, PLANE, 0, 0, tiled=True)  15.7 us
    ppermute x7, starting transfers between devices, shards(): send = lambda x, by: lax.ppermute(x, 'dir', neighbours(count, by))  13 us
    all_to_all x1, starting transfers between devices, shards(): gathered = lax.all_to_all(images, PLANE, 0, 0, tiled=True)  7.14 us
    ppermute x7, waiting for transfers between devices, shards(): send = lambda x, by: lax.ppermute(x, 'dir', neighbours(count, by))  6.83 us
    unnamed x14, local copies, waits for them, and re-layouts  2.98 us
    ppermute x1, starting transfers between devices, shards(): low = lax.ppermute(last, 'strip', neighbours(strips, 1))  2.61 us
    all_to_all x1, waiting for transfers between devices, shards(): gathered = lax.all_to_all(images, PLANE, 0, 0, tiled=True)  2.38 us
  transfers between devices with their start and end apart: 10, of which 4 were waited for; matrix products, arithmetic and copies ran while one was open for 0% of the time, Pallas kernels for 2%

profile of v2, /device:TPU:1, one launch (start us, length us, event | category | flops | bytes accessed | tf_op | source)
XLA Modules:
  0.0 98.1 jit_solution(17815763066279737192)
XLA Ops:
  0.7 1.2 %copy-done.2 = bf16[3,1,256,512]{3,2,1,0:T(8,128)(2,1)S(1)} copy-done((bf16[3,1,256,512]{3,2,1,0:T(8,128)(2,1)S(1)}, bf16[3,1,256,512]{3,2,1,0:T(8,128)(2,1)}, u32[]{:S(2)}) %copy-start.2) | copy-done | bytes 786456
  1.9 1.0 %copy-done.3 = f32[1,256,512]{2,1,0:T(8,128)S(1)} copy-done((f32[1,256,512]{2,1,0:T(8,128)S(1)}, f32[1,256,512]{2,1,0:T(8,128)}, u32[]{:S(2)}) %copy-start.3) | copy-done | bytes 524312
  2.9 0.7 copy-done.4
  3.6 0.1 ends.1
  3.7 2.6 %collective-permute-start = (f32[32,512]{1,0:T(8,128)S(1)}, f32[32,512]{1,0:T(8,128)S(1)}, u32[]{:S(2)}, u32[]{:S(2)}) collective-permute-start(f32[32,512]{1,0:T(8,128)S(1)} %get-tuple-element.29), channel_id=1, source_target_pairs={{0,8},{8,16},{16,24},{24,32},{32,40},{40,48},{48,56},{56,0},{1,9},... | collective-permute-start | bytes 196616 | tf_op jit(solution)/shard_map/ppermute | solution.py:266
  6.3 0.7 collective-permute-start.1
  7.6 2.1 %inner.1 = (bf16[3,256,512]{2,1,0:T(8,128)(2,1)S(1)}, f32[2,16,512]{2,1,0:T(8,128)S(1)}, bf16[2,3,32,512]{3,2,1,0:T(8,128)(2,1)S(1)}, f32[32,512]{1,0:T(8,128)S(...) custom-call(s32[1]{0:T(128)S(6)} %copy.12.wind, f32[256,512]{1,0:T(8,128)S(1)} %get-tuple-element.24.screen, ...), custom_call_target="tpu_custom_call" | custom-call | flops 4718592 | bytes 13107200 | tf_op jit(solution)/shard_map/inner/pallas_call | solution.py:269
  9.8 0.2 collective-permute-done.1.high
  10.0 2.3 %outer.1 = (f32[32,2,3,2,2,8,128]{6,5,4,3,2,1,0:T(8,128)}, f32[256,512]{1,0:T(8,128)}) custom-call(s32[1]{0:T(128)S(6)} %copy.12.wind, f32[2,16,512]{2,1,0:T(8,128)S(1)} %get-tuple-element.27.near0, bf16[2,3,32,512]{3,2,1,0:T(8,128)(2,1)S(1)} %get-tuple-element.28.fresh0, f32[32,512]{1,0:T(8,128)S(1)} %collective-permute-done.low, ...), custom_call_target="tpu_custom_call", output_to_operand_aliasing={{1}: (11, {})} | custom-call | tf_op jit(solution)/shard_map/outer/pallas_call | solution.py:304
  12.3 0.0 copy-start.5
  12.3 0.0 copy-start.6
  12.3 7.1 %all-to-all-start = ((f32[32,2,3,2,2,8,128]{6,5,4,3,2,1,0:T(8,128)}), f32[32,2,3,2,2,8,128]{6,5,4,3,2,1,0:T(8,128)S(1)}, u32[]{:S(2)}, u32[]{:S(2)}) async-start(f32[32,2,3,2,2,8,128]{6,5,4,3,2,1,0:T(8,128)} %get-tuple-element.37), calls=%async_computation | async-start | bytes 6291456 | tf_op jit(solution)/shard_map/all_to_all | solution.py:346
  19.5 0.2 slice_reduce_fusion
  19.8 36.4 %all-gather.1 = s32[4,2,8]{2,1,0:T(2,128)S(1)} all-gather(s32[1,2,8]{2,1,0:T(2,128)S(1)} %add_bitcast_fusion), channel_id=2, replica_groups=mesh['layer'=4,'strip'=8,'dir'=8] {'layer'}, dimensions={0}, use_global_device_ids=true | all-gather | bytes 320 | tf_op jit(solution)/shard_map/all_gather | solution.py:348
  56.2 0.1 reshape.14.places
  56.3 2.4 %all-to-all-done = f32[32,2,3,2,2,8,128]{6,5,4,3,2,1,0:T(8,128)S(1)} async-done(((f32[32,2,3,2,2,8,128]{6,5,4,3,2,1,0:T(8,128)}), f32[32,2,3,2,2,8,128]{6,5,4,3,2,1,0:T(8,128)S(1)}, u32[]{:S(2)}, u32[]{:S(2)}) %all-to-all-start) | async-done | bytes 3145760 | tf_op jit(solution)/shard_map/all_to_all | solution.py:346
  58.7 1.7 %feet.1 = f32[2,384,512]{2,1,0:T(8,128)S(1)} custom-call(s32[64]{0:T(128)S(1)} %reshape.14.places, f32[64,3,2,2,8,128]{5,4,3,2,1,0:T(8,128)S(1)} %bitcast.10), custom_call_target="tpu_custom_call" | custom-call | bytes 13107200 | tf_op jit(solution)/shard_map/feet/pallas_call | solution.py:350
  60.3 1.1 %pupil.1 = (f32[48,512]{1,0:T(8,128)S(1)}, f32[48,512]{1,0:T(8,128)S(1)}, f32[48,512]{1,0:T(8,128)S(1)}, f32[48,512]{1,0:T(8,128)S(1)}, f32[48,512]{1,0:T(8,128)...) custom-call(s32[1]{0:T(128)} %bitcast.4.mine, f32[2,384,512]{2,1,0:T(8,128)S(1)} %feet.1, ...), custom_call_target="tpu_custom_call" | custom-call | tf_op jit(solution)/shard_map/pupil/pallas_call | solution.py:359
  61.4 5.7 %collective-permute-start.5 = (f32[48,512]{1,0:T(8,128)S(1)}, f32[48,512]{1,0:T(8,128)S(1)}, u32[]{:S(2)}, u32[]{:S(2)}) collective-permute-start(f32[48,512]{1,0:T(8,128)S(1)} %get-tuple-element.43), channel_id=1, source_target_pairs={{0,7},{1,0},{2,1},{3,2},{4,3},{5,4},{6,5},{7,6},{8,15},{9,8},{10,9... | collective-permute-start | bytes 294920 | tf_op jit(solution)/shard_map/ppermute | solution.py:370
  67.1 1.2 %collective-permute-start.6 = (f32[48,512]{1,0:T(8,128)S(1)}, f32[48,512]{1,0:T(8,128)S(1)}, u32[]{:S(2)}, u32[]{:S(2)}) collective-permute-start(f32[48,512]{1,0:T(8,128)S(1)} %get-tuple-element.44), channel_id=1, source_target_pairs={{0,6},{1,7},{2,0},{3,1},{4,2},{5,3},{6,4},{7,5},{8,14},{9,15},{10,... | collective-permute-start | bytes 294920 | tf_op jit(solution)/shard_map/ppermute | solution.py:370
  68.2 0.7 collective-permute-start.2
  69.0 2.0 %collective-permute-start.3 = (f32[48,512]{1,0:T(8,128)S(1)}, f32[48,512]{1,0:T(8,128)S(1)}, u32[]{:S(2)}, u32[]{:S(2)}) collective-permute-start(f32[48,512]{1,0:T(8,128)S(1)} %get-tuple-element.40), channel_id=1, source_target_pairs={{0,7},{1,0},{2,1},{3,2},{4,3},{5,4},{6,5},{7,6},{8,15},{9,8},{10,9... | collective-permute-start | bytes 294920 | tf_op jit(solution)/shard_map/ppermute | solution.py:370
  70.9 0.0 collective-permute-done.5
  70.9 0.4 collective-permute-start.8
  71.3 0.2 collective-permute-done.6
  71.6 3.1 %collective-permute-start.7 = (f32[48,512]{1,0:T(8,128)S(1)}, f32[48,512]{1,0:T(8,128)S(1)}, u32[]{:S(2)}, u32[]{:S(2)}) collective-permute-start(f32[48,512]{1,0:T(8,128)S(1)} %add_add_fusion), channel_id=1, source_target_pairs={{0,6},{1,7},{2,0},{3,1},{4,2},{5,3},{6,4},{7,5},{8,14},{9,15},{10,... | collective-permute-start | bytes 294920 | tf_op jit(solution)/shard_map/ppermute | solution.py:370
  74.6 0.0 collective-permute-done.2.up1
  74.6 6.6 %collective-permute-done.4.up2 = f32[48,512]{1,0:T(8,128)S(1)} collective-permute-done((f32[48,512]{1,0:T(8,128)S(1)}, f32[48,512]{1,0:T(8,128)S(1)}, u32[]{:S(2)}, u32[]{:S(2)}) %collective-permute-start.4) | collective-permute-done | bytes 98336 | tf_op jit(solution)/shard_map/ppermute | solution.py:370
  81.2 0.0 collective-permute-done.8.up3
  81.2 0.3 pack.1
  81.6 15.7 %all_to_all.10.x = f32[32,8,128]{2,1,0:T(8,128)S(1)} all-to-all(f32[32,8,128]{2,1,0:T(8,128)S(1)} %pack.1), channel_id=1, replica_groups=mesh['layer'=4,'strip'=8,'dir'=8] {'layer','strip'}, dimensions={0} | all-to-all | bytes 262144 | tf_op jit(solution)/shard_map/all_to_all | solution.py:388
  97.3 0.8 slopes.1
  (15 shorter events, 0.1 us)
Async XLA Ops:
  0.6 9.4 %copy-start.1 = (bf16[2,512,512]{2,1,0:T(8,128)(2,1)S(1)}, bf16[2,512,512]{2,1,0:T(8,128)(2,1)}, u32[]{:S(2)}) copy-start(bf16[2,512,512]{2,1,0:T(8,128)(2,1)} %table.2) | copy-start | bytes 3145732
  0.6 1.2 %copy-start.2 = (bf16[3,1,256,512]{3,2,1,0:T(8,128)(2,1)S(1)}, bf16[3,1,256,512]{3,2,1,0:T(8,128)(2,1)}, u32[]{:S(2)}) copy-start(bf16[3,1,256,512]{3,2,1,0:T(8,128)(2,1)} %param.9) | copy-start | bytes 2359300
  1.9 1.0 %copy-start.3 = (f32[1,256,512]{2,1,0:T(8,128)S(1)}, f32[1,256,512]{2,1,0:T(8,128)}, u32[]{:S(2)}) copy-start(f32[1,256,512]{2,1,0:T(8,128)} %param.8) | copy-start | bytes 1572868
  2.9 0.7 copy-start.4
  3.7 6.1 %collective-permute-start = (f32[32,512]{1,0:T(8,128)S(1)}, f32[32,512]{1,0:T(8,128)S(1)}, u32[]{:S(2)}, u32[]{:S(2)}) collective-permute-start(f32[32,512]{1,0:T(8,128)S(1)} %get-tuple-element.29), channel_id=1, source_target_pairs={{0,8},{8,16},{16,24},{24,32},{32,40},{40,48},{48,56},{56,0},{1,9},... | collective-permute-start | bytes 196616 | tf_op jit(solution)/shard_map/ppermute | solution.py:266
  6.3 3.7 %collective-permute-start.1 = (f32[32,512]{1,0:T(8,128)S(1)}, f32[32,512]{1,0:T(8,128)S(1)}, u32[]{:S(2)}, u32[]{:S(2)}) collective-permute-start(f32[32,512]{1,0:T(8,128)S(1)} %get-tuple-element.30), channel_id=1, source_target_pairs={{0,56},{8,0},{16,8},{24,16},{32,24},{40,32},{48,40},{56,48},{1,57}... | collective-permute-start | bytes 196616 | tf_op jit(solution)/shard_map/ppermute | solution.py:267
  12.3 7.2 %copy-start.5 = (s32[8,1,32]{2,1,0:T(1,128)S(1)}, s32[8,1,32]{2,1,0:T(1,128)}, u32[]{:S(2)}) copy-start(s32[8,1,32]{2,1,0:T(1,128)} %param.12) | copy-start | bytes 3076
  12.3 7.4 %copy-start.6 = (s32[8,1]{0,1:T(1,128)S(1)}, s32[8,1]{0,1:T(1,128)}, u32[]{:S(2)}) copy-start(s32[8,1]{0,1:T(1,128)} %param.13) | copy-start | bytes 100
  12.3 46.3 %all-to-all-start = ((f32[32,2,3,2,2,8,128]{6,5,4,3,2,1,0:T(8,128)}), f32[32,2,3,2,2,8,128]{6,5,4,3,2,1,0:T(8,128)S(1)}, u32[]{:S(2)}, u32[]{:S(2)}) async-start(f32[32,2,3,2,2,8,128]{6,5,4,3,2,1,0:T(8,128)} %get-tuple-element.37), calls=%async_computation | async-start | bytes 6291456 | tf_op jit(solution)/shard_map/all_to_all | solution.py:346
  58.7 1.7 %copy-start = (bf16[2,512,512]{2,1,0:T(8,128)(2,1)S(1)}, bf16[2,512,512]{2,1,0:T(8,128)(2,1)}, u32[]{:S(2)}) copy-start(bf16[2,512,512]{2,1,0:T(8,128)(2,1)} %table.3) | copy-start | bytes 3145732
  61.4 9.5 %collective-permute-start.5 = (f32[48,512]{1,0:T(8,128)S(1)}, f32[48,512]{1,0:T(8,128)S(1)}, u32[]{:S(2)}, u32[]{:S(2)}) collective-permute-start(f32[48,512]{1,0:T(8,128)S(1)} %get-tuple-element.43), channel_id=1, source_target_pairs={{0,7},{1,0},{2,1},{3,2},{4,3},{5,4},{6,5},{7,6},{8,15},{9,8},{10,9... | collective-permute-start | bytes 294920 | tf_op jit(solution)/shard_map/ppermute | solution.py:370
  67.1 4.5 %collective-permute-start.6 = (f32[48,512]{1,0:T(8,128)S(1)}, f32[48,512]{1,0:T(8,128)S(1)}, u32[]{:S(2)}, u32[]{:S(2)}) collective-permute-start(f32[48,512]{1,0:T(8,128)S(1)} %get-tuple-element.44), channel_id=1, source_target_pairs={{0,6},{1,7},{2,0},{3,1},{4,2},{5,3},{6,4},{7,5},{8,14},{9,15},{10,... | collective-permute-start | bytes 294920 | tf_op jit(solution)/shard_map/ppermute | solution.py:370
  68.2 6.4 %collective-permute-start.2 = (f32[48,512]{1,0:T(8,128)S(1)}, f32[48,512]{1,0:T(8,128)S(1)}, u32[]{:S(2)}, u32[]{:S(2)}) collective-permute-start(f32[48,512]{1,0:T(8,128)S(1)} %get-tuple-element.39), channel_id=1, source_target_pairs={{0,1},{1,2},{2,3},{3,4},{4,5},{5,6},{6,7},{7,0},{8,9},{9,10},{10,1... | collective-permute-start | bytes 294920 | tf_op jit(solution)/shard_map/ppermute | solution.py:370
  69.0 5.7 %collective-permute-start.3 = (f32[48,512]{1,0:T(8,128)S(1)}, f32[48,512]{1,0:T(8,128)S(1)}, u32[]{:S(2)}, u32[]{:S(2)}) collective-permute-start(f32[48,512]{1,0:T(8,128)S(1)} %get-tuple-element.40), channel_id=1, source_target_pairs={{0,7},{1,0},{2,1},{3,2},{4,3},{5,4},{6,5},{7,6},{8,15},{9,8},{10,9... | collective-permute-start | bytes 294920 | tf_op jit(solution)/shard_map/ppermute | solution.py:370
  70.9 10.3 %collective-permute-start.4 = (f32[48,512]{1,0:T(8,128)S(1)}, f32[48,512]{1,0:T(8,128)S(1)}, u32[]{:S(2)}, u32[]{:S(2)}) collective-permute-start(f32[48,512]{1,0:T(8,128)S(1)} %get-tuple-element.41), channel_id=1, source_target_pairs={{0,2},{1,3},{2,4},{3,5},{4,6},{5,7},{6,0},{7,1},{8,10},{9,11},{10,... | collective-permute-start | bytes 294920 | tf_op jit(solution)/shard_map/ppermute | solution.py:370
  70.9 10.3 %collective-permute-start.8 = (f32[48,512]{1,0:T(8,128)S(1)}, f32[48,512]{1,0:T(8,128)S(1)}, u32[]{:S(2)}, u32[]{:S(2)}) collective-permute-start(f32[48,512]{1,0:T(8,128)S(1)} %get-tuple-element.45), channel_id=1, source_target_pairs={{0,3},{1,4},{2,5},{3,6},{4,7},{5,0},{6,1},{7,2},{8,11},{9,12},{10,... | collective-permute-start | bytes 294920 | tf_op jit(solution)/shard_map/ppermute | solution.py:370
  71.6 9.7 %collective-permute-start.7 = (f32[48,512]{1,0:T(8,128)S(1)}, f32[48,512]{1,0:T(8,128)S(1)}, u32[]{:S(2)}, u32[]{:S(2)}) collective-permute-start(f32[48,512]{1,0:T(8,128)S(1)} %add_add_fusion), channel_id=1, source_target_pairs={{0,6},{1,7},{2,0},{3,1},{4,2},{5,3},{6,4},{7,5},{8,14},{9,15},{10,... | collective-permute-start | bytes 294920 | tf_op jit(solution)/shard_map/ppermute | solution.py:370

commit v3 on v2

--- a/solution.py
+++ b/solution.py
@@ -32,7 +32,7 @@
     return total
 
 
-def ends_kernel(screen, fresh, coef, begin, last, screen_on, fresh_on, coef_on):
+def ends_kernel(screen, fresh, begin, last, screen_on, fresh_on):
     begin[0:16, :] = screen[0:16, :]
     last[0:16, :] = screen[ROWS - 16 : ROWS, :]
     for t in range(2):
@@ -41,13 +41,13 @@
         last[at, :] = fresh[t, ROWS - 16 : ROWS, :].astype(jnp.float32)[8:16, :]
     screen_on[...] = screen[...]
     fresh_on[...] = fresh[...]
-    coef_on[...] = coef[...]
 
 
 def inner_kernel(
-    wind, screen, fresh, coef, flats, near0, fresh0, near1, near2, near3, s3, s1, s2
+    wind, screen, fresh, coef, flats, near0, fresh0, near1, near2, near3, coef_on, s3, s1, s2
 ):
     shift = wind[0] + 2
+    coef_on[...] = coef[...]
     near0[0] = screen[0:16, :]
     near0[1] = screen[ROWS - 16 : ROWS, :]
     fresh0[0] = fresh[:, 0:32, :]
@@ -55,9 +55,13 @@
     steps = ((screen, s1, near1, 16, 16), (s1, s2, near2, 16, 16), (s2, s3, near3, 8, 32))
     for t, (src, dst, near, count, flat) in enumerate(steps):
         begin, end = 8 * (t + 1), ROWS - 8 * (t + 1)
-        for r in range(begin, end, 32):
-            stop = min(r + 32, end)
-            dst[r:stop, :] = advance(src[r - 8 : stop + 8, :], fresh[t, r:stop, :], coef, shift)
+        for r in range(begin, end, 64):
+            stop = min(r + 64, end)
+            for c in range(0, COLS, LANES):
+                at = slice(c, c + LANES)
+                dst[r:stop, at] = advance(
+                    src[r - 8 : stop + 8, at], fresh[t, r:stop, at], coef[:, :, at], shift
+                )
         near[0:count, :] = dst[begin : begin + count, :]
         near[count:, :] = dst[end - count : end, :]
         for r in range(flat, ROWS - flat, 32):
@@ -89,6 +93,8 @@
     none = jnp.zeros((8, COLS), jnp.float32)
     join = lambda *rows: jnp.concatenate(rows, axis=0)
     after = lambda window, fresh: advance(window, fresh, coef, shift)
+    leave = []
+
     def project(t):
         for m in range(NM):
             image = lax.dot_general(
@@ -97,10 +103,10 @@
             for half in range(2):
                 for part in range(2):
                     at = image[half * 256 : half * 256 + 256, part * LANES : part * LANES + LANES]
-                    piece[t, :, part, m, half, :, :] = at.reshape(CHUNKS, 8, LANES)
-        copy = pltpu.make_async_copy(piece.at[t], images.at[:, :, t], sem.at[t])
-        copy.start()
-        return copy
+                    piece[t, m, :, part, half, :, :] = at.reshape(CHUNKS, 8, LANES)
+            copy = pltpu.make_async_copy(piece.at[t, m], images.at[:, :, t, m], sem.at[NM * t + m])
+            copy.start()
+            leave.append(copy)
 
     first, final = fresh0[0, 0].astype(jnp.float32), fresh0[1, 0].astype(jnp.float32)
     e = after(join(low[0:16, :], near0[0]), join(low[16:24, :], first[0:8]))
@@ -108,7 +114,7 @@
     flat[0] = inside[0]
     flat[0, 0:16, :] = join(e[8:16], near1[0:8, :]).astype(jnp.bfloat16)
     flat[0, ROWS - 16 : ROWS, :] = join(near1[24:32, :], f[0:8]).astype(jnp.bfloat16)
-    leave = [project(0)]
+    project(0)
 
     first, final = fresh0[0, 1].astype(jnp.float32), fresh0[1, 1].astype(jnp.float32)
     e = after(join(none, e, near1[0:16, :]), join(low[24:32, :], first[0:16]))
@@ -116,7 +122,7 @@
     flat[1] = inside[1]
     flat[1, 0:16, :] = e[8:24].astype(jnp.bfloat16)
     flat[1, ROWS - 16 : ROWS, :] = f[0:16].astype(jnp.bfloat16)
-    leave.append(project(1))
+    project(1)
 
     first, final = fresh0[0, 2].astype(jnp.float32), fresh0[1, 2].astype(jnp.float32)
     e = after(join(e, near2[0:16, :]), first[0:24])
@@ -124,15 +130,15 @@
     ends[0] = e
     ends[1] = f
     leave += [
-        pltpu.make_async_copy(ends.at[0], screen_out.at[pl.ds(0, 24), :], sem.at[3]),
-        pltpu.make_async_copy(ends.at[1], screen_out.at[pl.ds(ROWS - 24, 24), :], sem.at[4]),
+        pltpu.make_async_copy(ends.at[0], screen_out.at[pl.ds(0, 24), :], sem.at[6]),
+        pltpu.make_async_copy(ends.at[1], screen_out.at[pl.ds(ROWS - 24, 24), :], sem.at[7]),
     ]
     leave[-2].start()
     leave[-1].start()
     flat[2] = inside[2]
     flat[2, 0:32, :] = join(e, near3[0:8, :]).astype(jnp.bfloat16)
     flat[2, ROWS - 32 : ROWS, :] = join(near3[8:16, :], f).astype(jnp.bfloat16)
-    leave.append(project(2))
+    project(2)
     for copy in leave:
         copy.wait()
 
@@ -243,26 +249,24 @@
 
     near = jax.ShapeDtypeStruct((32, COLS), jnp.float32)
     taps = jax.ShapeDtypeStruct((TAPS, 1, COLS), jnp.float32)
-    begin, last, state, fresh, taps = pl.pallas_call(
+    begin, last, state, fresh = pl.pallas_call(
         ends_kernel,
-        in_specs=[whole(ROWS, COLS), whole(STEPS, ROWS, COLS), whole(TAPS, 1, COLS)],
+        in_specs=[whole(ROWS, COLS), whole(STEPS, ROWS, COLS)],
         out_specs=[
             whole(32, COLS),
             whole(32, COLS),
             whole(ROWS, COLS),
             whole(STEPS, ROWS, COLS),
-            whole(TAPS, 1, COLS),
         ],
         out_shape=[
             near,
             near,
             jax.ShapeDtypeStruct((ROWS, COLS), jnp.float32),
             jax.ShapeDtypeStruct((STEPS, ROWS, COLS), jnp.bfloat16),
-            taps,
         ],
         compiler_params=room(24),
         name="ends",
-    )(state, fresh, jnp.swapaxes(coef, 0, 1))
+    )(state, fresh)
     low = lax.ppermute(last, "strip", neighbours(strips, 1))
     high = lax.ppermute(begin, "strip", neighbours(strips, -1))
 
@@ -281,6 +285,7 @@
             whole(32, COLS),
             whole(32, COLS),
             whole(16, COLS),
+            whole(TAPS, 1, COLS),
             whole(ROWS, COLS),
         ],
         out_shape=[
@@ -290,6 +295,7 @@
             near,
             near,
             jax.ShapeDtypeStruct((16, COLS), jnp.float32),
+            taps,
             jax.ShapeDtypeStruct((ROWS, COLS), jnp.float32),
         ],
         scratch_shapes=[pltpu.VMEM((ROWS, COLS), jnp.float32)] * 2,
@@ -298,7 +304,7 @@
             flops=12 * STEPS * ROWS * COLS, bytes_accessed=100 * ROWS * COLS, transcendentals=0
         ),
         name="inner",
-    )(wind, state, fresh, taps)
+    )(wind, state, fresh, jnp.swapaxes(coef, 0, 1))
 
     anywhere = pl.BlockSpec(memory_space=pl.ANY)
     images, screen_out = pl.pallas_call(
@@ -325,9 +331,9 @@
         input_output_aliases={11: 1},
         scratch_shapes=[
             pltpu.VMEM((STEPS, ROWS, COLS), jnp.bfloat16),
-            pltpu.VMEM((STEPS, CHUNKS, 2, NM, 2, 8, LANES), jnp.float32),
+            pltpu.VMEM((STEPS, NM, CHUNKS, 2, 2, 8, LANES), jnp.float32),
             pltpu.VMEM((2, 24, COLS), jnp.float32),
-            pltpu.SemaphoreType.DMA((5,)),
+            pltpu.SemaphoreType.DMA((8,)),
         ],
         compiler_params=room(50),
         name="outer",
@@ -336,7 +342,7 @@
         *inside[1:3],
         low,
         high,
-        taps,
+        inside[6],
         *inside[3:6],
         column_table,
         inside[0],
@@ -369,12 +375,12 @@
     count = lax.axis_size("dir")
     send = lambda x, by: lax.ppermute(x, "dir", neighbours(count, by))
     far = send(pupils[4], -2)
+    down3 = send(pupils[5], -2)
     up3 = send(pupils[3], 3)
-    down3 = send(pupils[5], -1)
     up2 = send(pupils[2], 2)
-    down1 = send(pupils[7], -1)
     up1 = send(pupils[1], 1)
-    down2 = send(pupils[6] + down3 + far, -2)
+    down2 = send(pupils[6] + far, -2)
+    down1 = send(pupils[7] + down3, -1)
     terms = [pupils[0], up1, down1, up2, down2, up3]
 
     packed = pl.pallas_call(

time: 98.4 us -> 98.3 us (level)
  starting transfers between devices: 23.4 us -> 24.5 us
    ppermute x7, starting transfers between devices: 13 us -> 14.1 us  [shards(): send = lambda x, by: lax.ppermute(x, 'dir', neighbours(count, by))]
  transfers between devices with their start and end apart: 10 -> 10, of which waited for: 4 -> 3; matrix products, arithmetic and copies ran while one was open for 0% -> 0% of each run, Pallas kernels for 2% -> 2%
where the time goes in v3:
time: 98.3 us; the launch traced here: 98 us
  blocking collectives  51.7 us (53%)
  starting transfers between devices  24.5 us (25%)
  waiting for transfers between devices  8.6 us (9%)
  Pallas kernels  8.43 us (9%)
  local copies, waits for them, and re-layouts  3.29 us (3%)
  between operations  1.42 us (1%)
    all_gather x1, blocking collectives, shards(): places = lax.all_gather(places, 'layer').reshape(LAYERS * 2 * NDIR)  36.4 us
    all_to_all x1, blocking collectives, shards(): rows = lax.all_to_all(packed, PLANE, 0, 0, tiled=True)  15.3 us
    ppermute x7, starting transfers between devices, shards(): send = lambda x, by: lax.ppermute(x, 'dir', neighbours(count, by))  14.1 us
    all_to_all x1, starting transfers between devices, shards(): gathered = lax.all_to_all(images, PLANE, 0, 0, tiled=True)  7.06 us
    ppermute x7, waiting for transfers between devices, shards(): send = lambda x, by: lax.ppermute(x, 'dir', neighbours(count, by))  6.21 us
    unnamed x14, local copies, waits for them, and re-layouts  2.97 us
    ppermute x1, starting transfers between devices, shards(): low = lax.ppermute(last, 'strip', neighbours(strips, 1))  2.61 us
    all_to_all x1, waiting for transfers between devices, shards(): gathered = lax.all_to_all(images, PLANE, 0, 0, tiled=True)  2.38 us
  transfers between devices with their start and end apart: 10, of which 3 were waited for; matrix products, arithmetic and copies ran while one was open for 0% of the time, Pallas kernels for 2%

profile of v3, /device:TPU:1, one launch (start us, length us, event | category | flops | bytes accessed | tf_op | source)
XLA Modules:
  0.0 98.0 jit_solution(12060835060565296249)
XLA Ops:
  0.6 1.2 %copy-done.2 = bf16[3,1,256,512]{3,2,1,0:T(8,128)(2,1)S(1)} copy-done((bf16[3,1,256,512]{3,2,1,0:T(8,128)(2,1)S(1)}, bf16[3,1,256,512]{3,2,1,0:T(8,128)(2,1)}, u32[]{:S(2)}) %copy-start.2) | copy-done | bytes 786456
  1.9 1.0 %copy-done.3 = f32[1,256,512]{2,1,0:T(8,128)S(1)} copy-done((f32[1,256,512]{2,1,0:T(8,128)S(1)}, f32[1,256,512]{2,1,0:T(8,128)}, u32[]{:S(2)}) %copy-start.3) | copy-done | bytes 524312
  2.9 0.1 ends.1
  3.0 2.6 %collective-permute-start = (f32[32,512]{1,0:T(8,128)S(1)}, f32[32,512]{1,0:T(8,128)S(1)}, u32[]{:S(2)}, u32[]{:S(2)}) collective-permute-start(f32[32,512]{1,0:T(8,128)S(1)} %get-tuple-element.28), channel_id=1, source_target_pairs={{0,8},{8,16},{16,24},{24,32},{32,40},{40,48},{48,56},{56,0},{1,9},... | collective-permute-start | bytes 196616 | tf_op jit(solution)/shard_map/ppermute | solution.py:270
  5.6 0.7 collective-permute-start.1
  6.9 0.0 copy-start.4
  6.9 0.7 copy-done.4
  7.6 2.1 %inner.1 = (bf16[3,256,512]{2,1,0:T(8,128)(2,1)S(1)}, f32[2,16,512]{2,1,0:T(8,128)S(1)}, bf16[2,3,32,512]{3,2,1,0:T(8,128)(2,1)S(1)}, f32[32,512]{1,0:T(8,128)S(...) custom-call(s32[1]{0:T(128)S(6)} %copy.12.wind, ...), custom_call_target="tpu_custom_call" | custom-call | flops 4718592 | bytes 13107200 | tf_op jit(solution)/shard_map/inner/pallas_call | solution.py:273
  9.7 2.4 %outer.1 = (f32[32,2,3,2,2,8,128]{6,5,4,3,2,1,0:T(8,128)}, f32[256,512]{1,0:T(8,128)}) custom-call(s32[1]{0:T(128)S(6)} %copy.12.wind, f32[2,16,512]{2,1,0:T(8,128)S(1)} %get-tuple-element.26.near0, bf16[2,3,32,512]{3,2,1,0:T(8,128)(2,1)S(1)} %get-tuple-element.27.fresh0, f32[32,512]{1,0:T(8,128)S(1)} %collective-permute-done.low, ...), custom_call_target="tpu_custom_call", output_to_operand_aliasing={{1}: (11, {})} | custom-call | tf_op jit(solution)/shard_map/outer/pallas_call | solution.py:310
  12.1 0.0 copy-start.5
  12.1 0.0 copy-start.6
  12.1 7.1 %all-to-all-start = ((f32[32,2,3,2,2,8,128]{6,5,4,3,2,1,0:T(8,128)}), f32[32,2,3,2,2,8,128]{6,5,4,3,2,1,0:T(8,128)S(1)}, u32[]{:S(2)}, u32[]{:S(2)}) async-start(f32[32,2,3,2,2,8,128]{6,5,4,3,2,1,0:T(8,128)} %get-tuple-element.37), calls=%async_computation | async-start | bytes 6291456 | tf_op jit(solution)/shard_map/all_to_all | solution.py:352
  19.2 0.2 slice_reduce_fusion
  19.5 36.4 %all-gather.1 = s32[4,2,8]{2,1,0:T(2,128)S(1)} all-gather(s32[1,2,8]{2,1,0:T(2,128)S(1)} %add_bitcast_fusion), channel_id=2, replica_groups=mesh['layer'=4,'strip'=8,'dir'=8] {'layer'}, dimensions={0}, use_global_device_ids=true | all-gather | bytes 320 | tf_op jit(solution)/shard_map/all_gather | solution.py:354
  55.9 0.1 reshape.14.places
  56.0 2.4 %all-to-all-done = f32[32,2,3,2,2,8,128]{6,5,4,3,2,1,0:T(8,128)S(1)} async-done(((f32[32,2,3,2,2,8,128]{6,5,4,3,2,1,0:T(8,128)}), f32[32,2,3,2,2,8,128]{6,5,4,3,2,1,0:T(8,128)S(1)}, u32[]{:S(2)}, u32[]{:S(2)}) %all-to-all-start) | async-done | bytes 3145760 | tf_op jit(solution)/shard_map/all_to_all | solution.py:352
  58.4 1.7 %feet.1 = f32[2,384,512]{2,1,0:T(8,128)S(1)} custom-call(s32[64]{0:T(128)S(1)} %reshape.14.places, f32[64,3,2,2,8,128]{5,4,3,2,1,0:T(8,128)S(1)} %bitcast.10), custom_call_target="tpu_custom_call" | custom-call | bytes 13107200 | tf_op jit(solution)/shard_map/feet/pallas_call | solution.py:356
  60.0 1.1 %pupil.1 = (f32[48,512]{1,0:T(8,128)S(1)}, f32[48,512]{1,0:T(8,128)S(1)}, f32[48,512]{1,0:T(8,128)S(1)}, f32[48,512]{1,0:T(8,128)S(1)}, f32[48,512]{1,0:T(8,128)...) custom-call(s32[1]{0:T(128)} %bitcast.4.mine, f32[2,384,512]{2,1,0:T(8,128)S(1)} %feet.1, ...), custom_call_target="tpu_custom_call" | custom-call | tf_op jit(solution)/shard_map/pupil/pallas_call | solution.py:365
  61.1 6.1 %collective-permute-start.6 = (f32[48,512]{1,0:T(8,128)S(1)}, f32[48,512]{1,0:T(8,128)S(1)}, u32[]{:S(2)}, u32[]{:S(2)}) collective-permute-start(f32[48,512]{1,0:T(8,128)S(1)} %get-tuple-element.44), channel_id=1, source_target_pairs={{0,6},{1,7},{2,0},{3,1},{4,2},{5,3},{6,4},{7,5},{8,14},{9,15},{10,... | collective-permute-start | bytes 294920 | tf_op jit(solution)/shard_map/ppermute | solution.py:376
  67.2 1.2 %collective-permute-start.3 = (f32[48,512]{1,0:T(8,128)S(1)}, f32[48,512]{1,0:T(8,128)S(1)}, u32[]{:S(2)}, u32[]{:S(2)}) collective-permute-start(f32[48,512]{1,0:T(8,128)S(1)} %get-tuple-element.41), channel_id=1, source_target_pairs={{0,6},{1,7},{2,0},{3,1},{4,2},{5,3},{6,4},{7,5},{8,14},{9,15},{10,... | collective-permute-start | bytes 294920 | tf_op jit(solution)/shard_map/ppermute | solution.py:376
  68.4 0.7 collective-permute-start.2
  69.1 1.2 %collective-permute-start.5 = (f32[48,512]{1,0:T(8,128)S(1)}, f32[48,512]{1,0:T(8,128)S(1)}, u32[]{:S(2)}, u32[]{:S(2)}) collective-permute-start(f32[48,512]{1,0:T(8,128)S(1)} %get-tuple-element.42), channel_id=1, source_target_pairs={{0,2},{1,3},{2,4},{3,5},{4,6},{5,7},{6,0},{7,1},{8,10},{9,11},{10,... | collective-permute-start | bytes 294920 | tf_op jit(solution)/shard_map/ppermute | solution.py:376
  70.3 0.5 collective-permute-start.8
  70.9 0.0 collective-permute-done.6
  70.9 4.1 %collective-permute-start.7 = (f32[48,512]{1,0:T(8,128)S(1)}, f32[48,512]{1,0:T(8,128)S(1)}, u32[]{:S(2)}, u32[]{:S(2)}) collective-permute-start(f32[48,512]{1,0:T(8,128)S(1)} %add.7), channel_id=1, source_target_pairs={{0,6},{1,7},{2,0},{3,1},{4,2},{5,3},{6,4},{7,5},{8,14},{9,15},{10,... | collective-permute-start | bytes 294920 | tf_op jit(solution)/shard_map/ppermute | solution.py:376
  75.0 0.0 collective-permute-done.3
  75.0 0.3 collective-permute-start.4
  75.3 1.5 %collective-permute-done.5.up2 = f32[48,512]{1,0:T(8,128)S(1)} collective-permute-done((f32[48,512]{1,0:T(8,128)S(1)}, f32[48,512]{1,0:T(8,128)S(1)}, u32[]{:S(2)}, u32[]{:S(2)}) %collective-permute-start.5) | collective-permute-done | bytes 98336 | tf_op jit(solution)/shard_map/ppermute | solution.py:376
  76.8 4.7 %collective-permute-done.8.up3 = f32[48,512]{1,0:T(8,128)S(1)} collective-permute-done((f32[48,512]{1,0:T(8,128)S(1)}, f32[48,512]{1,0:T(8,128)S(1)}, u32[]{:S(2)}, u32[]{:S(2)}) %collective-permute-start.8) | collective-permute-done | bytes 98336 | tf_op jit(solution)/shard_map/ppermute | solution.py:376
  81.5 0.3 pack.1
  81.8 15.3 %all_to_all.10.x = f32[32,8,128]{2,1,0:T(8,128)S(1)} all-to-all(f32[32,8,128]{2,1,0:T(8,128)S(1)} %pack.1), channel_id=1, replica_groups=mesh['layer'=4,'strip'=8,'dir'=8] {'layer','strip'}, dimensions={0} | all-to-all | bytes 262144 | tf_op jit(solution)/shard_map/all_to_all | solution.py:394
  97.1 0.8 slopes.1
  (16 shorter events, 0.1 us)
Async XLA Ops:
  0.6 9.1 %copy-start.1 = (bf16[2,512,512]{2,1,0:T(8,128)(2,1)S(1)}, bf16[2,512,512]{2,1,0:T(8,128)(2,1)}, u32[]{:S(2)}) copy-start(bf16[2,512,512]{2,1,0:T(8,128)(2,1)} %table.2) | copy-start | bytes 3145732
  0.6 1.2 %copy-start.2 = (bf16[3,1,256,512]{3,2,1,0:T(8,128)(2,1)S(1)}, bf16[3,1,256,512]{3,2,1,0:T(8,128)(2,1)}, u32[]{:S(2)}) copy-start(bf16[3,1,256,512]{3,2,1,0:T(8,128)(2,1)} %param.9) | copy-start | bytes 2359300
  1.9 1.0 %copy-start.3 = (f32[1,256,512]{2,1,0:T(8,128)S(1)}, f32[1,256,512]{2,1,0:T(8,128)}, u32[]{:S(2)}) copy-start(f32[1,256,512]{2,1,0:T(8,128)} %param.8) | copy-start | bytes 1572868
  3.0 6.7 %collective-permute-start = (f32[32,512]{1,0:T(8,128)S(1)}, f32[32,512]{1,0:T(8,128)S(1)}, u32[]{:S(2)}, u32[]{:S(2)}) collective-permute-start(f32[32,512]{1,0:T(8,128)S(1)} %get-tuple-element.28), channel_id=1, source_target_pairs={{0,8},{8,16},{16,24},{24,32},{32,40},{40,48},{48,56},{56,0},{1,9},... | collective-permute-start | bytes 196616 | tf_op jit(solution)/shard_map/ppermute | solution.py:270
  5.6 4.1 %collective-permute-start.1 = (f32[32,512]{1,0:T(8,128)S(1)}, f32[32,512]{1,0:T(8,128)S(1)}, u32[]{:S(2)}, u32[]{:S(2)}) collective-permute-start(f32[32,512]{1,0:T(8,128)S(1)} %get-tuple-element.29), channel_id=1, source_target_pairs={{0,56},{8,0},{16,8},{24,16},{32,24},{40,32},{48,40},{56,48},{1,57}... | collective-permute-start | bytes 196616 | tf_op jit(solution)/shard_map/ppermute | solution.py:271
  6.9 0.7 copy-start.4
  12.1 7.1 %copy-start.5 = (s32[8,1,32]{2,1,0:T(1,128)S(1)}, s32[8,1,32]{2,1,0:T(1,128)}, u32[]{:S(2)}) copy-start(s32[8,1,32]{2,1,0:T(1,128)} %param.12) | copy-start | bytes 3076
  12.1 7.3 %copy-start.6 = (s32[8,1]{0,1:T(1,128)S(1)}, s32[8,1]{0,1:T(1,128)}, u32[]{:S(2)}) copy-start(s32[8,1]{0,1:T(1,128)} %param.13) | copy-start | bytes 100
  12.1 46.2 %all-to-all-start = ((f32[32,2,3,2,2,8,128]{6,5,4,3,2,1,0:T(8,128)}), f32[32,2,3,2,2,8,128]{6,5,4,3,2,1,0:T(8,128)S(1)}, u32[]{:S(2)}, u32[]{:S(2)}) async-start(f32[32,2,3,2,2,8,128]{6,5,4,3,2,1,0:T(8,128)} %get-tuple-element.37), calls=%async_computation | async-start | bytes 6291456 | tf_op jit(solution)/shard_map/all_to_all | solution.py:352
  58.4 1.7 %copy-start = (bf16[2,512,512]{2,1,0:T(8,128)(2,1)S(1)}, bf16[2,512,512]{2,1,0:T(8,128)(2,1)}, u32[]{:S(2)}) copy-start(bf16[2,512,512]{2,1,0:T(8,128)(2,1)} %table.3) | copy-start | bytes 3145732
  61.1 9.7 %collective-permute-start.6 = (f32[48,512]{1,0:T(8,128)S(1)}, f32[48,512]{1,0:T(8,128)S(1)}, u32[]{:S(2)}, u32[]{:S(2)}) collective-permute-start(f32[48,512]{1,0:T(8,128)S(1)} %get-tuple-element.44), channel_id=1, source_target_pairs={{0,6},{1,7},{2,0},{3,1},{4,2},{5,3},{6,4},{7,5},{8,14},{9,15},{10,... | collective-permute-start | bytes 294920 | tf_op jit(solution)/shard_map/ppermute | solution.py:376
  67.2 7.7 %collective-permute-start.3 = (f32[48,512]{1,0:T(8,128)S(1)}, f32[48,512]{1,0:T(8,128)S(1)}, u32[]{:S(2)}, u32[]{:S(2)}) collective-permute-start(f32[48,512]{1,0:T(8,128)S(1)} %get-tuple-element.41), channel_id=1, source_target_pairs={{0,6},{1,7},{2,0},{3,1},{4,2},{5,3},{6,4},{7,5},{8,14},{9,15},{10,... | collective-permute-start | bytes 294920 | tf_op jit(solution)/shard_map/ppermute | solution.py:376
  68.4 6.9 %collective-permute-start.2 = (f32[48,512]{1,0:T(8,128)S(1)}, f32[48,512]{1,0:T(8,128)S(1)}, u32[]{:S(2)}, u32[]{:S(2)}) collective-permute-start(f32[48,512]{1,0:T(8,128)S(1)} %get-tuple-element.39), channel_id=1, source_target_pairs={{0,1},{1,2},{2,3},{3,4},{4,5},{5,6},{6,7},{7,0},{8,9},{9,10},{10,1... | collective-permute-start | bytes 294920 | tf_op jit(solution)/shard_map/ppermute | solution.py:376
  69.1 7.7 %collective-permute-start.5 = (f32[48,512]{1,0:T(8,128)S(1)}, f32[48,512]{1,0:T(8,128)S(1)}, u32[]{:S(2)}, u32[]{:S(2)}) collective-permute-start(f32[48,512]{1,0:T(8,128)S(1)} %get-tuple-element.42), channel_id=1, source_target_pairs={{0,2},{1,3},{2,4},{3,5},{4,6},{5,7},{6,0},{7,1},{8,10},{9,11},{10,... | collective-permute-start | bytes 294920 | tf_op jit(solution)/shard_map/ppermute | solution.py:376
  70.3 11.2 %collective-permute-start.8 = (f32[48,512]{1,0:T(8,128)S(1)}, f32[48,512]{1,0:T(8,128)S(1)}, u32[]{:S(2)}, u32[]{:S(2)}) collective-permute-start(f32[48,512]{1,0:T(8,128)S(1)} %get-tuple-element.45), channel_id=1, source_target_pairs={{0,3},{1,4},{2,5},{3,6},{4,7},{5,0},{6,1},{7,2},{8,11},{9,12},{10,... | collective-permute-start | bytes 294920 | tf_op jit(solution)/shard_map/ppermute | solution.py:376
  70.9 10.6 %collective-permute-start.7 = (f32[48,512]{1,0:T(8,128)S(1)}, f32[48,512]{1,0:T(8,128)S(1)}, u32[]{:S(2)}, u32[]{:S(2)}) collective-permute-start(f32[48,512]{1,0:T(8,128)S(1)} %add.7), channel_id=1, source_target_pairs={{0,6},{1,7},{2,0},{3,1},{4,2},{5,3},{6,4},{7,5},{8,14},{9,15},{10,... | collective-permute-start | bytes 294920 | tf_op jit(solution)/shard_map/ppermute | solution.py:376
  75.0 6.5 %collective-permute-start.4 = (f32[48,512]{1,0:T(8,128)S(1)}, f32[48,512]{1,0:T(8,128)S(1)}, u32[]{:S(2)}, u32[]{:S(2)}) collective-permute-start(f32[48,512]{1,0:T(8,128)S(1)} %add.6), channel_id=1, source_target_pairs={{0,7},{1,0},{2,1},{3,2},{4,3},{5,4},{6,5},{7,6},{8,15},{9,8},{10,9... | collective-permute-start | bytes 294920 | tf_op jit(solution)/shard_map/ppermute | solution.py:376

commit v4 on v3

--- a/solution.py
+++ b/solution.py
@@ -59,8 +59,10 @@
             stop = min(r + 64, end)
             for c in range(0, COLS, LANES):
                 at = slice(c, c + LANES)
+                low, high = r // 16 * 16, -(-stop // 16) * 16
+                rows = fresh[t, low:high, at].astype(jnp.float32)[r - low : stop - low]
                 dst[r:stop, at] = advance(
-                    src[r - 8 : stop + 8, at], fresh[t, r:stop, at], coef[:, :, at], shift
+                    src[r - 8 : stop + 8, at], rows, coef[:, :, at], shift
                 )
         near[0:count, :] = dst[begin : begin + count, :]
         near[count:, :] = dst[end - count : end, :]

time: 98.3 us -> 98.3 us (level)
  no operation moved by 1% of the time
where the time goes in v4:
time: 98.3 us; the launch traced here: 98 us
  blocking collectives  51.6 us (52%)
  starting transfers between devices  24.5 us (25%)
  waiting for transfers between devices  8.77 us (9%)
  Pallas kernels  8.44 us (9%)
  local copies, waits for them, and re-layouts  3.29 us (3%)
  between operations  1.42 us (1%)
    all_gather x1, blocking collectives, shards(): places = lax.all_gather(places, 'layer').reshape(LAYERS * 2 * NDIR)  36.4 us
    all_to_all x1, blocking collectives, shards(): rows = lax.all_to_all(packed, PLANE, 0, 0, tiled=True)  15.1 us
    ppermute x7, starting transfers between devices, shards(): send = lambda x, by: lax.ppermute(x, 'dir', neighbours(count, by))  14.1 us
    all_to_all x1, starting transfers between devices, shards(): gathered = lax.all_to_all(images, PLANE, 0, 0, tiled=True)  7.08 us
    ppermute x7, waiting for transfers between devices, shards(): send = lambda x, by: lax.ppermute(x, 'dir', neighbours(count, by))  6.38 us
    unnamed x14, local copies, waits for them, and re-layouts  2.97 us
    ppermute x1, starting transfers between devices, shards(): low = lax.ppermute(last, 'strip', neighbours(strips, 1))  2.61 us
    all_to_all x1, waiting for transfers between devices, shards(): gathered = lax.all_to_all(images, PLANE, 0, 0, tiled=True)  2.38 us
  transfers between devices with their start and end apart: 10, of which 3 were waited for; matrix products, arithmetic and copies ran while one was open for 0% of the time, Pallas kernels for 2%

profile of v4, /device:TPU:1, one launch (start us, length us, event | category | flops | bytes accessed | tf_op | source)
XLA Modules:
  0.0 98.0 jit_solution(6753416165467494743)
XLA Ops:
  0.6 1.2 %copy-done.2 = bf16[3,1,256,512]{3,2,1,0:T(8,128)(2,1)S(1)} copy-done((bf16[3,1,256,512]{3,2,1,0:T(8,128)(2,1)S(1)}, bf16[3,1,256,512]{3,2,1,0:T(8,128)(2,1)}, u32[]{:S(2)}) %copy-start.2) | copy-done | bytes 786456
  1.9 1.0 %copy-done.3 = f32[1,256,512]{2,1,0:T(8,128)S(1)} copy-done((f32[1,256,512]{2,1,0:T(8,128)S(1)}, f32[1,256,512]{2,1,0:T(8,128)}, u32[]{:S(2)}) %copy-start.3) | copy-done | bytes 524312
  2.9 0.1 ends.1
  3.0 2.6 %collective-permute-start = (f32[32,512]{1,0:T(8,128)S(1)}, f32[32,512]{1,0:T(8,128)S(1)}, u32[]{:S(2)}, u32[]{:S(2)}) collective-permute-start(f32[32,512]{1,0:T(8,128)S(1)} %get-tuple-element.28), channel_id=1, source_target_pairs={{0,8},{8,16},{16,24},{24,32},{32,40},{40,48},{48,56},{56,0},{1,9},... | collective-permute-start | bytes 196616 | tf_op jit(solution)/shard_map/ppermute | solution.py:272
  5.6 0.7 collective-permute-start.1
  6.9 0.0 copy-start.4
  6.9 0.7 copy-done.4
  7.6 2.1 %inner.1 = (bf16[3,256,512]{2,1,0:T(8,128)(2,1)S(1)}, f32[2,16,512]{2,1,0:T(8,128)S(1)}, bf16[2,3,32,512]{3,2,1,0:T(8,128)(2,1)S(1)}, f32[32,512]{1,0:T(8,128)S(...) custom-call(s32[1]{0:T(128)S(6)} %copy.12.wind, ...), custom_call_target="tpu_custom_call" | custom-call | flops 4718592 | bytes 13107200 | tf_op jit(solution)/shard_map/inner/pallas_call | solution.py:275
  9.7 0.0 collective-permute-done.1.high
  9.7 2.4 %outer.1 = (f32[32,2,3,2,2,8,128]{6,5,4,3,2,1,0:T(8,128)}, f32[256,512]{1,0:T(8,128)}) custom-call(s32[1]{0:T(128)S(6)} %copy.12.wind, f32[2,16,512]{2,1,0:T(8,128)S(1)} %get-tuple-element.26.near0, bf16[2,3,32,512]{3,2,1,0:T(8,128)(2,1)S(1)} %get-tuple-element.27.fresh0, f32[32,512]{1,0:T(8,128)S(1)} %collective-permute-done.low, ...), custom_call_target="tpu_custom_call", output_to_operand_aliasing={{1}: (11, {})} | custom-call | tf_op jit(solution)/shard_map/outer/pallas_call | solution.py:312
  12.1 0.0 copy-start.5
  12.1 0.0 copy-start.6
  12.1 7.1 %all-to-all-start = ((f32[32,2,3,2,2,8,128]{6,5,4,3,2,1,0:T(8,128)}), f32[32,2,3,2,2,8,128]{6,5,4,3,2,1,0:T(8,128)S(1)}, u32[]{:S(2)}, u32[]{:S(2)}) async-start(f32[32,2,3,2,2,8,128]{6,5,4,3,2,1,0:T(8,128)} %get-tuple-element.37), calls=%async_computation | async-start | bytes 6291456 | tf_op jit(solution)/shard_map/all_to_all | solution.py:354
  19.2 0.2 slice_reduce_fusion
  19.5 36.4 %all-gather.1 = s32[4,2,8]{2,1,0:T(2,128)S(1)} all-gather(s32[1,2,8]{2,1,0:T(2,128)S(1)} %add_bitcast_fusion), channel_id=2, replica_groups=mesh['layer'=4,'strip'=8,'dir'=8] {'layer'}, dimensions={0}, use_global_device_ids=true | all-gather | bytes 320 | tf_op jit(solution)/shard_map/all_gather | solution.py:356
  55.9 0.1 reshape.14.places
  56.0 2.4 %all-to-all-done = f32[32,2,3,2,2,8,128]{6,5,4,3,2,1,0:T(8,128)S(1)} async-done(((f32[32,2,3,2,2,8,128]{6,5,4,3,2,1,0:T(8,128)}), f32[32,2,3,2,2,8,128]{6,5,4,3,2,1,0:T(8,128)S(1)}, u32[]{:S(2)}, u32[]{:S(2)}) %all-to-all-start) | async-done | bytes 3145760 | tf_op jit(solution)/shard_map/all_to_all | solution.py:354
  58.4 1.7 %feet.1 = f32[2,384,512]{2,1,0:T(8,128)S(1)} custom-call(s32[64]{0:T(128)S(1)} %reshape.14.places, f32[64,3,2,2,8,128]{5,4,3,2,1,0:T(8,128)S(1)} %bitcast.10), custom_call_target="tpu_custom_call" | custom-call | bytes 13107200 | tf_op jit(solution)/shard_map/feet/pallas_call | solution.py:358
  60.1 1.1 %pupil.1 = (f32[48,512]{1,0:T(8,128)S(1)}, f32[48,512]{1,0:T(8,128)S(1)}, f32[48,512]{1,0:T(8,128)S(1)}, f32[48,512]{1,0:T(8,128)S(1)}, f32[48,512]{1,0:T(8,128)...) custom-call(s32[1]{0:T(128)} %bitcast.4.mine, f32[2,384,512]{2,1,0:T(8,128)S(1)} %feet.1, ...), custom_call_target="tpu_custom_call" | custom-call | tf_op jit(solution)/shard_map/pupil/pallas_call | solution.py:367
  61.1 6.1 %collective-permute-start.6 = (f32[48,512]{1,0:T(8,128)S(1)}, f32[48,512]{1,0:T(8,128)S(1)}, u32[]{:S(2)}, u32[]{:S(2)}) collective-permute-start(f32[48,512]{1,0:T(8,128)S(1)} %get-tuple-element.44), channel_id=1, source_target_pairs={{0,6},{1,7},{2,0},{3,1},{4,2},{5,3},{6,4},{7,5},{8,14},{9,15},{10,... | collective-permute-start | bytes 294920 | tf_op jit(solution)/shard_map/ppermute | solution.py:378
  67.2 1.2 %collective-permute-start.3 = (f32[48,512]{1,0:T(8,128)S(1)}, f32[48,512]{1,0:T(8,128)S(1)}, u32[]{:S(2)}, u32[]{:S(2)}) collective-permute-start(f32[48,512]{1,0:T(8,128)S(1)} %get-tuple-element.41), channel_id=1, source_target_pairs={{0,6},{1,7},{2,0},{3,1},{4,2},{5,3},{6,4},{7,5},{8,14},{9,15},{10,... | collective-permute-start | bytes 294920 | tf_op jit(solution)/shard_map/ppermute | solution.py:378
  68.4 0.7 collective-permute-start.2
  69.2 1.2 %collective-permute-start.5 = (f32[48,512]{1,0:T(8,128)S(1)}, f32[48,512]{1,0:T(8,128)S(1)}, u32[]{:S(2)}, u32[]{:S(2)}) collective-permute-start(f32[48,512]{1,0:T(8,128)S(1)} %get-tuple-element.42), channel_id=1, source_target_pairs={{0,2},{1,3},{2,4},{3,5},{4,6},{5,7},{6,0},{7,1},{8,10},{9,11},{10,... | collective-permute-start | bytes 294920 | tf_op jit(solution)/shard_map/ppermute | solution.py:378
  70.3 0.5 collective-permute-start.8
  70.9 4.2 %collective-permute-start.7 = (f32[48,512]{1,0:T(8,128)S(1)}, f32[48,512]{1,0:T(8,128)S(1)}, u32[]{:S(2)}, u32[]{:S(2)}) collective-permute-start(f32[48,512]{1,0:T(8,128)S(1)} %add.7), channel_id=1, source_target_pairs={{0,6},{1,7},{2,0},{3,1},{4,2},{5,3},{6,4},{7,5},{8,14},{9,15},{10,... | collective-permute-start | bytes 294920 | tf_op jit(solution)/shard_map/ppermute | solution.py:378
  75.1 0.0 collective-permute-done.3
  75.1 0.2 collective-permute-start.4
  75.3 1.6 %collective-permute-done.5.up2 = f32[48,512]{1,0:T(8,128)S(1)} collective-permute-done((f32[48,512]{1,0:T(8,128)S(1)}, f32[48,512]{1,0:T(8,128)S(1)}, u32[]{:S(2)}, u32[]{:S(2)}) %collective-permute-start.5) | collective-permute-done | bytes 98336 | tf_op jit(solution)/shard_map/ppermute | solution.py:378
  76.9 4.8 %collective-permute-done.8.up3 = f32[48,512]{1,0:T(8,128)S(1)} collective-permute-done((f32[48,512]{1,0:T(8,128)S(1)}, f32[48,512]{1,0:T(8,128)S(1)}, u32[]{:S(2)}, u32[]{:S(2)}) %collective-permute-start.8) | collective-permute-done | bytes 98336 | tf_op jit(solution)/shard_map/ppermute | solution.py:378
  81.7 0.3 pack.1
  82.0 15.1 %all_to_all.10.x = f32[32,8,128]{2,1,0:T(8,128)S(1)} all-to-all(f32[32,8,128]{2,1,0:T(8,128)S(1)} %pack.1), channel_id=1, replica_groups=mesh['layer'=4,'strip'=8,'dir'=8] {'layer','strip'}, dimensions={0} | all-to-all | bytes 262144 | tf_op jit(solution)/shard_map/all_to_all | solution.py:396
  97.1 0.8 slopes.1
  (16 shorter events, 0.1 us)
Async XLA Ops:
  0.6 9.1 %copy-start.1 = (bf16[2,512,512]{2,1,0:T(8,128)(2,1)S(1)}, bf16[2,512,512]{2,1,0:T(8,128)(2,1)}, u32[]{:S(2)}) copy-start(bf16[2,512,512]{2,1,0:T(8,128)(2,1)} %table.2) | copy-start | bytes 3145732
  0.6 1.2 %copy-start.2 = (bf16[3,1,256,512]{3,2,1,0:T(8,128)(2,1)S(1)}, bf16[3,1,256,512]{3,2,1,0:T(8,128)(2,1)}, u32[]{:S(2)}) copy-start(bf16[3,1,256,512]{3,2,1,0:T(8,128)(2,1)} %param.9) | copy-start | bytes 2359300
  1.9 1.0 %copy-start.3 = (f32[1,256,512]{2,1,0:T(8,128)S(1)}, f32[1,256,512]{2,1,0:T(8,128)}, u32[]{:S(2)}) copy-start(f32[1,256,512]{2,1,0:T(8,128)} %param.8) | copy-start | bytes 1572868
  3.0 6.7 %collective-permute-start = (f32[32,512]{1,0:T(8,128)S(1)}, f32[32,512]{1,0:T(8,128)S(1)}, u32[]{:S(2)}, u32[]{:S(2)}) collective-permute-start(f32[32,512]{1,0:T(8,128)S(1)} %get-tuple-element.28), channel_id=1, source_target_pairs={{0,8},{8,16},{16,24},{24,32},{32,40},{40,48},{48,56},{56,0},{1,9},... | collective-permute-start | bytes 196616 | tf_op jit(solution)/shard_map/ppermute | solution.py:272
  5.6 4.1 %collective-permute-start.1 = (f32[32,512]{1,0:T(8,128)S(1)}, f32[32,512]{1,0:T(8,128)S(1)}, u32[]{:S(2)}, u32[]{:S(2)}) collective-permute-start(f32[32,512]{1,0:T(8,128)S(1)} %get-tuple-element.29), channel_id=1, source_target_pairs={{0,56},{8,0},{16,8},{24,16},{32,24},{40,32},{48,40},{56,48},{1,57}... | collective-permute-start | bytes 196616 | tf_op jit(solution)/shard_map/ppermute | solution.py:273
  6.9 0.7 copy-start.4
  12.1 7.1 %copy-start.5 = (s32[8,1,32]{2,1,0:T(1,128)S(1)}, s32[8,1,32]{2,1,0:T(1,128)}, u32[]{:S(2)}) copy-start(s32[8,1,32]{2,1,0:T(1,128)} %param.12) | copy-start | bytes 3076
  12.1 7.3 %copy-start.6 = (s32[8,1]{0,1:T(1,128)S(1)}, s32[8,1]{0,1:T(1,128)}, u32[]{:S(2)}) copy-start(s32[8,1]{0,1:T(1,128)} %param.13) | copy-start | bytes 100
  12.1 46.3 %all-to-all-start = ((f32[32,2,3,2,2,8,128]{6,5,4,3,2,1,0:T(8,128)}), f32[32,2,3,2,2,8,128]{6,5,4,3,2,1,0:T(8,128)S(1)}, u32[]{:S(2)}, u32[]{:S(2)}) async-start(f32[32,2,3,2,2,8,128]{6,5,4,3,2,1,0:T(8,128)} %get-tuple-element.37), calls=%async_computation | async-start | bytes 6291456 | tf_op jit(solution)/shard_map/all_to_all | solution.py:354
  58.4 1.7 %copy-start = (bf16[2,512,512]{2,1,0:T(8,128)(2,1)S(1)}, bf16[2,512,512]{2,1,0:T(8,128)(2,1)}, u32[]{:S(2)}) copy-start(bf16[2,512,512]{2,1,0:T(8,128)(2,1)} %table.3) | copy-start | bytes 3145732
  61.1 9.7 %collective-permute-start.6 = (f32[48,512]{1,0:T(8,128)S(1)}, f32[48,512]{1,0:T(8,128)S(1)}, u32[]{:S(2)}, u32[]{:S(2)}) collective-permute-start(f32[48,512]{1,0:T(8,128)S(1)} %get-tuple-element.44), channel_id=1, source_target_pairs={{0,6},{1,7},{2,0},{3,1},{4,2},{5,3},{6,4},{7,5},{8,14},{9,15},{10,... | collective-permute-start | bytes 294920 | tf_op jit(solution)/shard_map/ppermute | solution.py:378
  67.2 7.9 %collective-permute-start.3 = (f32[48,512]{1,0:T(8,128)S(1)}, f32[48,512]{1,0:T(8,128)S(1)}, u32[]{:S(2)}, u32[]{:S(2)}) collective-permute-start(f32[48,512]{1,0:T(8,128)S(1)} %get-tuple-element.41), channel_id=1, source_target_pairs={{0,6},{1,7},{2,0},{3,1},{4,2},{5,3},{6,4},{7,5},{8,14},{9,15},{10,... | collective-permute-start | bytes 294920 | tf_op jit(solution)/shard_map/ppermute | solution.py:378
  68.4 6.9 %collective-permute-start.2 = (f32[48,512]{1,0:T(8,128)S(1)}, f32[48,512]{1,0:T(8,128)S(1)}, u32[]{:S(2)}, u32[]{:S(2)}) collective-permute-start(f32[48,512]{1,0:T(8,128)S(1)} %get-tuple-element.39), channel_id=1, source_target_pairs={{0,1},{1,2},{2,3},{3,4},{4,5},{5,6},{6,7},{7,0},{8,9},{9,10},{10,1... | collective-permute-start | bytes 294920 | tf_op jit(solution)/shard_map/ppermute | solution.py:378
  69.2 7.7 %collective-permute-start.5 = (f32[48,512]{1,0:T(8,128)S(1)}, f32[48,512]{1,0:T(8,128)S(1)}, u32[]{:S(2)}, u32[]{:S(2)}) collective-permute-start(f32[48,512]{1,0:T(8,128)S(1)} %get-tuple-element.42), channel_id=1, source_target_pairs={{0,2},{1,3},{2,4},{3,5},{4,6},{5,7},{6,0},{7,1},{8,10},{9,11},{10,... | collective-permute-start | bytes 294920 | tf_op jit(solution)/shard_map/ppermute | solution.py:378
  70.3 11.3 %collective-permute-start.8 = (f32[48,512]{1,0:T(8,128)S(1)}, f32[48,512]{1,0:T(8,128)S(1)}, u32[]{:S(2)}, u32[]{:S(2)}) collective-permute-start(f32[48,512]{1,0:T(8,128)S(1)} %get-tuple-element.45), channel_id=1, source_target_pairs={{0,3},{1,4},{2,5},{3,6},{4,7},{5,0},{6,1},{7,2},{8,11},{9,12},{10,... | collective-permute-start | bytes 294920 | tf_op jit(solution)/shard_map/ppermute | solution.py:378
  70.9 10.8 %collective-permute-start.7 = (f32[48,512]{1,0:T(8,128)S(1)}, f32[48,512]{1,0:T(8,128)S(1)}, u32[]{:S(2)}, u32[]{:S(2)}) collective-permute-start(f32[48,512]{1,0:T(8,128)S(1)} %add.7), channel_id=1, source_target_pairs={{0,6},{1,7},{2,0},{3,1},{4,2},{5,3},{6,4},{7,5},{8,14},{9,15},{10,... | collective-permute-start | bytes 294920 | tf_op jit(solution)/shard_map/ppermute | solution.py:378
  75.1 6.6 %collective-permute-start.4 = (f32[48,512]{1,0:T(8,128)S(1)}, f32[48,512]{1,0:T(8,128)S(1)}, u32[]{:S(2)}, u32[]{:S(2)}) collective-permute-start(f32[48,512]{1,0:T(8,128)S(1)} %add.6), channel_id=1, source_target_pairs={{0,7},{1,0},{2,1},{3,2},{4,3},{5,4},{6,5},{7,6},{8,15},{9,8},{10,9... | collective-permute-start | bytes 294920 | tf_op jit(solution)/shard_map/ppermute | solution.py:378

commit v5 on v4

--- a/solution.py
+++ b/solution.py
@@ -33,12 +33,14 @@
 
 
 def ends_kernel(screen, fresh, begin, last, screen_on, fresh_on):
-    begin[0:16, :] = screen[0:16, :]
-    last[0:16, :] = screen[ROWS - 16 : ROWS, :]
-    for t in range(2):
-        at = slice(16 + 8 * t, 24 + 8 * t)
-        begin[at, :] = fresh[t, 0:16, :].astype(jnp.float32)[0:8, :]
-        last[at, :] = fresh[t, ROWS - 16 : ROWS, :].astype(jnp.float32)[8:16, :]
+    row = lax.broadcasted_iota(jnp.int32, (16, COLS), 0)
+    first, final = fresh[1, 0:16, :], fresh[1, ROWS - 16 : ROWS, :]
+    first = pltpu.roll(first.astype(jnp.float32), 12, axis=0)
+    final = pltpu.roll(final.astype(jnp.float32), 4, axis=0)
+    begin[0:16, :] = jnp.where(row < 12, screen[0:16, :], first)
+    last[0:16, :] = jnp.where(row < 4, final, screen[ROWS - 16 : ROWS, :])
+    begin[16:24, :] = fresh[0, 0:16, :].astype(jnp.float32)[0:8, :]
+    last[16:24, :] = fresh[0, ROWS - 16 : ROWS, :].astype(jnp.float32)[8:16, :]
     screen_on[...] = screen[...]
     fresh_on[...] = fresh[...]
 
@@ -119,8 +121,8 @@
     project(0)
 
     first, final = fresh0[0, 1].astype(jnp.float32), fresh0[1, 1].astype(jnp.float32)
-    e = after(join(none, e, near1[0:16, :]), join(low[24:32, :], first[0:16]))
-    f = after(join(near1[16:32, :], f, none), join(final[16:32], high[24:32, :]))
+    e = after(join(none, e, near1[0:16, :]), join(pltpu.roll(low[0:8, :], 4, axis=0), first[0:16]))
+    f = after(join(near1[16:32, :], f, none), join(final[16:32], pltpu.roll(high[8:16, :], 4, axis=0)))
     flat[1] = inside[1]
     flat[1, 0:16, :] = e[8:24].astype(jnp.bfloat16)
     flat[1, ROWS - 16 : ROWS, :] = f[0:16].astype(jnp.bfloat16)
@@ -249,20 +251,21 @@
     fresh = innovation[:, 0]
     strips = lax.axis_size("strip")
 
+    halo = jax.ShapeDtypeStruct((24, COLS), jnp.float32)
     near = jax.ShapeDtypeStruct((32, COLS), jnp.float32)
     taps = jax.ShapeDtypeStruct((TAPS, 1, COLS), jnp.float32)
     begin, last, state, fresh = pl.pallas_call(
         ends_kernel,
         in_specs=[whole(ROWS, COLS), whole(STEPS, ROWS, COLS)],
         out_specs=[
-            whole(32, COLS),
-            whole(32, COLS),
+            whole(24, COLS),
+            whole(24, COLS),
             whole(ROWS, COLS),
             whole(STEPS, ROWS, COLS),
         ],
         out_shape=[
-            near,
-            near,
+            halo,
+            halo,
             jax.ShapeDtypeStruct((ROWS, COLS), jnp.float32),
             jax.ShapeDtypeStruct((STEPS, ROWS, COLS), jnp.bfloat16),
         ],
@@ -315,8 +318,8 @@
             SCALARS,
             whole(2, 16, COLS),
             whole(2, STEPS, 32, COLS),
-            whole(32, COLS),
-            whole(32, COLS),
+            whole(24, COLS),
+            whole(24, COLS),
             whole(TAPS, 1, COLS),
             whole(32, COLS),
             whole(32, COLS),

time: 98.3 us -> 98.3 us (level)
  no operation moved by 1% of the time
where the time goes in v5:
time: 98.3 us; the launch traced here: 98 us
  blocking collectives  51.7 us (53%)
  starting transfers between devices  24.5 us (25%)
  waiting for transfers between devices  8.6 us (9%)
  Pallas kernels  8.43 us (9%)
  local copies, waits for them, and re-layouts  3.29 us (3%)
  between operations  1.42 us (1%)
    all_gather x1, blocking collectives, shards(): places = lax.all_gather(places, 'layer').reshape(LAYERS * 2 * NDIR)  36.4 us
    all_to_all x1, blocking collectives, shards(): rows = lax.all_to_all(packed, PLANE, 0, 0, tiled=True)  15.3 us
    ppermute x7, starting transfers between devices, shards(): send = lambda x, by: lax.ppermute(x, 'dir', neighbours(count, by))  14.1 us
    all_to_all x1, starting transfers between devices, shards(): gathered = lax.all_to_all(images, PLANE, 0, 0, tiled=True)  7.07 us
    ppermute x7, waiting for transfers between devices, shards(): send = lambda x, by: lax.ppermute(x, 'dir', neighbours(count, by))  6.21 us
    unnamed x14, local copies, waits for them, and re-layouts  2.97 us
    ppermute x1, starting transfers between devices, shards(): low = lax.ppermute(last, 'strip', neighbours(strips, 1))  2.61 us
    all_to_all x1, waiting for transfers between devices, shards(): gathered = lax.all_to_all(images, PLANE, 0, 0, tiled=True)  2.38 us
  transfers between devices with their start and end apart: 10, of which 3 were waited for; matrix products, arithmetic and copies ran while one was open for 0% of the time, Pallas kernels for 2%

profile of v5, /device:TPU:1, one launch (start us, length us, event | category | flops | bytes accessed | tf_op | source)
XLA Modules:
  0.0 98.0 jit_solution(15339046492891412131)
XLA Ops:
  0.6 1.2 %copy-done.2 = bf16[3,1,256,512]{3,2,1,0:T(8,128)(2,1)S(1)} copy-done((bf16[3,1,256,512]{3,2,1,0:T(8,128)(2,1)S(1)}, bf16[3,1,256,512]{3,2,1,0:T(8,128)(2,1)}, u32[]{:S(2)}) %copy-start.2) | copy-done | bytes 786456
  1.9 1.0 %copy-done.3 = f32[1,256,512]{2,1,0:T(8,128)S(1)} copy-done((f32[1,256,512]{2,1,0:T(8,128)S(1)}, f32[1,256,512]{2,1,0:T(8,128)}, u32[]{:S(2)}) %copy-start.3) | copy-done | bytes 524312
  2.9 0.1 ends.1
  3.0 2.6 %collective-permute-start = (f32[24,512]{1,0:T(8,128)S(1)}, f32[24,512]{1,0:T(8,128)S(1)}, u32[]{:S(2)}, u32[]{:S(2)}) collective-permute-start(f32[24,512]{1,0:T(8,128)S(1)} %get-tuple-element.28), channel_id=1, source_target_pairs={{0,8},{8,16},{16,24},{24,32},{32,40},{40,48},{48,56},{56,0},{1,9},... | collective-permute-start | bytes 147464 | tf_op jit(solution)/shard_map/ppermute | solution.py:275
  5.6 0.7 collective-permute-start.1
  6.9 0.0 copy-start.4
  6.9 0.7 copy-done.4
  7.6 2.1 %inner.1 = (bf16[3,256,512]{2,1,0:T(8,128)(2,1)S(1)}, f32[2,16,512]{2,1,0:T(8,128)S(1)}, bf16[2,3,32,512]{3,2,1,0:T(8,128)(2,1)S(1)}, f32[32,512]{1,0:T(8,128)S(...) custom-call(s32[1]{0:T(128)S(6)} %copy.12.wind, ...), custom_call_target="tpu_custom_call" | custom-call | flops 4718592 | bytes 13107200 | tf_op jit(solution)/shard_map/inner/pallas_call | solution.py:278
  9.7 0.0 collective-permute-done.low
  9.7 0.0 collective-permute-done.1.high
  9.7 2.4 %outer.1 = (f32[32,2,3,2,2,8,128]{6,5,4,3,2,1,0:T(8,128)}, f32[256,512]{1,0:T(8,128)}) custom-call(s32[1]{0:T(128)S(6)} %copy.12.wind, f32[2,16,512]{2,1,0:T(8,128)S(1)} %get-tuple-element.26.near0, bf16[2,3,32,512]{3,2,1,0:T(8,128)(2,1)S(1)} %get-tuple-element.27.fresh0, f32[24,512]{1,0:T(8,128)S(1)} %collective-permute-done.low, ...), custom_call_target="tpu_custom_call", output_to_operand_aliasing={{1}: (11, {})} | custom-call | tf_op jit(solution)/shard_map/outer/pallas_call | solution.py:315
  12.1 0.0 copy-start.5
  12.1 0.0 copy-start.6
  12.1 7.1 %all-to-all-start = ((f32[32,2,3,2,2,8,128]{6,5,4,3,2,1,0:T(8,128)}), f32[32,2,3,2,2,8,128]{6,5,4,3,2,1,0:T(8,128)S(1)}, u32[]{:S(2)}, u32[]{:S(2)}) async-start(f32[32,2,3,2,2,8,128]{6,5,4,3,2,1,0:T(8,128)} %get-tuple-element.37), calls=%async_computation | async-start | bytes 6291456 | tf_op jit(solution)/shard_map/all_to_all | solution.py:357
  19.2 0.2 slice_reduce_fusion
  19.4 36.4 %all-gather.1 = s32[4,2,8]{2,1,0:T(2,128)S(1)} all-gather(s32[1,2,8]{2,1,0:T(2,128)S(1)} %add_bitcast_fusion), channel_id=2, replica_groups=mesh['layer'=4,'strip'=8,'dir'=8] {'layer'}, dimensions={0}, use_global_device_ids=true | all-gather | bytes 320 | tf_op jit(solution)/shard_map/all_gather | solution.py:359
  55.9 0.1 reshape.14.places
  56.0 2.4 %all-to-all-done = f32[32,2,3,2,2,8,128]{6,5,4,3,2,1,0:T(8,128)S(1)} async-done(((f32[32,2,3,2,2,8,128]{6,5,4,3,2,1,0:T(8,128)}), f32[32,2,3,2,2,8,128]{6,5,4,3,2,1,0:T(8,128)S(1)}, u32[]{:S(2)}, u32[]{:S(2)}) %all-to-all-start) | async-done | bytes 3145760 | tf_op jit(solution)/shard_map/all_to_all | solution.py:357
  58.3 1.7 %feet.1 = f32[2,384,512]{2,1,0:T(8,128)S(1)} custom-call(s32[64]{0:T(128)S(1)} %reshape.14.places, f32[64,3,2,2,8,128]{5,4,3,2,1,0:T(8,128)S(1)} %bitcast.10), custom_call_target="tpu_custom_call" | custom-call | bytes 13107200 | tf_op jit(solution)/shard_map/feet/pallas_call | solution.py:361
  60.0 1.1 %pupil.1 = (f32[48,512]{1,0:T(8,128)S(1)}, f32[48,512]{1,0:T(8,128)S(1)}, f32[48,512]{1,0:T(8,128)S(1)}, f32[48,512]{1,0:T(8,128)S(1)}, f32[48,512]{1,0:T(8,128)...) custom-call(s32[1]{0:T(128)} %bitcast.4.mine, f32[2,384,512]{2,1,0:T(8,128)S(1)} %feet.1, ...), custom_call_target="tpu_custom_call" | custom-call | tf_op jit(solution)/shard_map/pupil/pallas_call | solution.py:370
  61.1 6.1 %collective-permute-start.6 = (f32[48,512]{1,0:T(8,128)S(1)}, f32[48,512]{1,0:T(8,128)S(1)}, u32[]{:S(2)}, u32[]{:S(2)}) collective-permute-start(f32[48,512]{1,0:T(8,128)S(1)} %get-tuple-element.44), channel_id=1, source_target_pairs={{0,6},{1,7},{2,0},{3,1},{4,2},{5,3},{6,4},{7,5},{8,14},{9,15},{10,... | collective-permute-start | bytes 294920 | tf_op jit(solution)/shard_map/ppermute | solution.py:381
  67.2 1.2 %collective-permute-start.3 = (f32[48,512]{1,0:T(8,128)S(1)}, f32[48,512]{1,0:T(8,128)S(1)}, u32[]{:S(2)}, u32[]{:S(2)}) collective-permute-start(f32[48,512]{1,0:T(8,128)S(1)} %get-tuple-element.41), channel_id=1, source_target_pairs={{0,6},{1,7},{2,0},{3,1},{4,2},{5,3},{6,4},{7,5},{8,14},{9,15},{10,... | collective-permute-start | bytes 294920 | tf_op jit(solution)/shard_map/ppermute | solution.py:381
  68.4 0.7 collective-permute-start.2
  69.1 1.2 %collective-permute-start.5 = (f32[48,512]{1,0:T(8,128)S(1)}, f32[48,512]{1,0:T(8,128)S(1)}, u32[]{:S(2)}, u32[]{:S(2)}) collective-permute-start(f32[48,512]{1,0:T(8,128)S(1)} %get-tuple-element.42), channel_id=1, source_target_pairs={{0,2},{1,3},{2,4},{3,5},{4,6},{5,7},{6,0},{7,1},{8,10},{9,11},{10,... | collective-permute-start | bytes 294920 | tf_op jit(solution)/shard_map/ppermute | solution.py:381
  70.3 0.5 collective-permute-start.8
  70.9 4.1 %collective-permute-start.7 = (f32[48,512]{1,0:T(8,128)S(1)}, f32[48,512]{1,0:T(8,128)S(1)}, u32[]{:S(2)}, u32[]{:S(2)}) collective-permute-start(f32[48,512]{1,0:T(8,128)S(1)} %add.7), channel_id=1, source_target_pairs={{0,6},{1,7},{2,0},{3,1},{4,2},{5,3},{6,4},{7,5},{8,14},{9,15},{10,... | collective-permute-start | bytes 294920 | tf_op jit(solution)/shard_map/ppermute | solution.py:381
  75.0 0.3 collective-permute-start.4
  75.3 1.5 %collective-permute-done.5.up2 = f32[48,512]{1,0:T(8,128)S(1)} collective-permute-done((f32[48,512]{1,0:T(8,128)S(1)}, f32[48,512]{1,0:T(8,128)S(1)}, u32[]{:S(2)}, u32[]{:S(2)}) %collective-permute-start.5) | collective-permute-done | bytes 98336 | tf_op jit(solution)/shard_map/ppermute | solution.py:381
  76.8 4.7 %collective-permute-done.8.up3 = f32[48,512]{1,0:T(8,128)S(1)} collective-permute-done((f32[48,512]{1,0:T(8,128)S(1)}, f32[48,512]{1,0:T(8,128)S(1)}, u32[]{:S(2)}, u32[]{:S(2)}) %collective-permute-start.8) | collective-permute-done | bytes 98336 | tf_op jit(solution)/shard_map/ppermute | solution.py:381
  81.5 0.3 pack.1
  81.8 15.3 %all_to_all.10.x = f32[32,8,128]{2,1,0:T(8,128)S(1)} all-to-all(f32[32,8,128]{2,1,0:T(8,128)S(1)} %pack.1), channel_id=1, replica_groups=mesh['layer'=4,'strip'=8,'dir'=8] {'layer','strip'}, dimensions={0} | all-to-all | bytes 262144 | tf_op jit(solution)/shard_map/all_to_all | solution.py:399
  97.1 0.8 slopes.1
  (16 shorter events, 0.1 us)
Async XLA Ops:
  0.6 9.1 %copy-start.1 = (bf16[2,512,512]{2,1,0:T(8,128)(2,1)S(1)}, bf16[2,512,512]{2,1,0:T(8,128)(2,1)}, u32[]{:S(2)}) copy-start(bf16[2,512,512]{2,1,0:T(8,128)(2,1)} %table.2) | copy-start | bytes 3145732
  0.6 1.2 %copy-start.2 = (bf16[3,1,256,512]{3,2,1,0:T(8,128)(2,1)S(1)}, bf16[3,1,256,512]{3,2,1,0:T(8,128)(2,1)}, u32[]{:S(2)}) copy-start(bf16[3,1,256,512]{3,2,1,0:T(8,128)(2,1)} %param.9) | copy-start | bytes 2359300
  1.9 1.0 %copy-start.3 = (f32[1,256,512]{2,1,0:T(8,128)S(1)}, f32[1,256,512]{2,1,0:T(8,128)}, u32[]{:S(2)}) copy-start(f32[1,256,512]{2,1,0:T(8,128)} %param.8) | copy-start | bytes 1572868
  3.0 6.7 %collective-permute-start = (f32[24,512]{1,0:T(8,128)S(1)}, f32[24,512]{1,0:T(8,128)S(1)}, u32[]{:S(2)}, u32[]{:S(2)}) collective-permute-start(f32[24,512]{1,0:T(8,128)S(1)} %get-tuple-element.28), channel_id=1, source_target_pairs={{0,8},{8,16},{16,24},{24,32},{32,40},{40,48},{48,56},{56,0},{1,9},... | collective-permute-start | bytes 147464 | tf_op jit(solution)/shard_map/ppermute | solution.py:275
  5.6 4.1 %collective-permute-start.1 = (f32[24,512]{1,0:T(8,128)S(1)}, f32[24,512]{1,0:T(8,128)S(1)}, u32[]{:S(2)}, u32[]{:S(2)}) collective-permute-start(f32[24,512]{1,0:T(8,128)S(1)} %get-tuple-element.29), channel_id=1, source_target_pairs={{0,56},{8,0},{16,8},{24,16},{32,24},{40,32},{48,40},{56,48},{1,57}... | collective-permute-start | bytes 147464 | tf_op jit(solution)/shard_map/ppermute | solution.py:276
  6.9 0.7 copy-start.4
  12.1 7.1 %copy-start.5 = (s32[8,1,32]{2,1,0:T(1,128)S(1)}, s32[8,1,32]{2,1,0:T(1,128)}, u32[]{:S(2)}) copy-start(s32[8,1,32]{2,1,0:T(1,128)} %param.12) | copy-start | bytes 3076
  12.1 7.3 %copy-start.6 = (s32[8,1]{0,1:T(1,128)S(1)}, s32[8,1]{0,1:T(1,128)}, u32[]{:S(2)}) copy-start(s32[8,1]{0,1:T(1,128)} %param.13) | copy-start | bytes 100
  12.1 46.2 %all-to-all-start = ((f32[32,2,3,2,2,8,128]{6,5,4,3,2,1,0:T(8,128)}), f32[32,2,3,2,2,8,128]{6,5,4,3,2,1,0:T(8,128)S(1)}, u32[]{:S(2)}, u32[]{:S(2)}) async-start(f32[32,2,3,2,2,8,128]{6,5,4,3,2,1,0:T(8,128)} %get-tuple-element.37), calls=%async_computation | async-start | bytes 6291456 | tf_op jit(solution)/shard_map/all_to_all | solution.py:357
  58.3 1.7 %copy-start = (bf16[2,512,512]{2,1,0:T(8,128)(2,1)S(1)}, bf16[2,512,512]{2,1,0:T(8,128)(2,1)}, u32[]{:S(2)}) copy-start(bf16[2,512,512]{2,1,0:T(8,128)(2,1)} %table.3) | copy-start | bytes 3145732
  61.1 9.7 %collective-permute-start.6 = (f32[48,512]{1,0:T(8,128)S(1)}, f32[48,512]{1,0:T(8,128)S(1)}, u32[]{:S(2)}, u32[]{:S(2)}) collective-permute-start(f32[48,512]{1,0:T(8,128)S(1)} %get-tuple-element.44), channel_id=1, source_target_pairs={{0,6},{1,7},{2,0},{3,1},{4,2},{5,3},{6,4},{7,5},{8,14},{9,15},{10,... | collective-permute-start | bytes 294920 | tf_op jit(solution)/shard_map/ppermute | solution.py:381
  67.2 7.8 %collective-permute-start.3 = (f32[48,512]{1,0:T(8,128)S(1)}, f32[48,512]{1,0:T(8,128)S(1)}, u32[]{:S(2)}, u32[]{:S(2)}) collective-permute-start(f32[48,512]{1,0:T(8,128)S(1)} %get-tuple-element.41), channel_id=1, source_target_pairs={{0,6},{1,7},{2,0},{3,1},{4,2},{5,3},{6,4},{7,5},{8,14},{9,15},{10,... | collective-permute-start | bytes 294920 | tf_op jit(solution)/shard_map/ppermute | solution.py:381
  68.4 6.9 %collective-permute-start.2 = (f32[48,512]{1,0:T(8,128)S(1)}, f32[48,512]{1,0:T(8,128)S(1)}, u32[]{:S(2)}, u32[]{:S(2)}) collective-permute-start(f32[48,512]{1,0:T(8,128)S(1)} %get-tuple-element.39), channel_id=1, source_target_pairs={{0,1},{1,2},{2,3},{3,4},{4,5},{5,6},{6,7},{7,0},{8,9},{9,10},{10,1... | collective-permute-start | bytes 294920 | tf_op jit(solution)/shard_map/ppermute | solution.py:381
  69.1 7.7 %collective-permute-start.5 = (f32[48,512]{1,0:T(8,128)S(1)}, f32[48,512]{1,0:T(8,128)S(1)}, u32[]{:S(2)}, u32[]{:S(2)}) collective-permute-start(f32[48,512]{1,0:T(8,128)S(1)} %get-tuple-element.42), channel_id=1, source_target_pairs={{0,2},{1,3},{2,4},{3,5},{4,6},{5,7},{6,0},{7,1},{8,10},{9,11},{10,... | collective-permute-start | bytes 294920 | tf_op jit(solution)/shard_map/ppermute | solution.py:381
  70.3 11.2 %collective-permute-start.8 = (f32[48,512]{1,0:T(8,128)S(1)}, f32[48,512]{1,0:T(8,128)S(1)}, u32[]{:S(2)}, u32[]{:S(2)}) collective-permute-start(f32[48,512]{1,0:T(8,128)S(1)} %get-tuple-element.45), channel_id=1, source_target_pairs={{0,3},{1,4},{2,5},{3,6},{4,7},{5,0},{6,1},{7,2},{8,11},{9,12},{10,... | collective-permute-start | bytes 294920 | tf_op jit(solution)/shard_map/ppermute | solution.py:381
  70.9 10.6 %collective-permute-start.7 = (f32[48,512]{1,0:T(8,128)S(1)}, f32[48,512]{1,0:T(8,128)S(1)}, u32[]{:S(2)}, u32[]{:S(2)}) collective-permute-start(f32[48,512]{1,0:T(8,128)S(1)} %add.7), channel_id=1, source_target_pairs={{0,6},{1,7},{2,0},{3,1},{4,2},{5,3},{6,4},{7,5},{8,14},{9,15},{10,... | collective-permute-start | bytes 294920 | tf_op jit(solution)/shard_map/ppermute | solution.py:381
  75.0 6.5 %collective-permute-start.4 = (f32[48,512]{1,0:T(8,128)S(1)}, f32[48,512]{1,0:T(8,128)S(1)}, u32[]{:S(2)}, u32[]{:S(2)}) collective-permute-start(f32[48,512]{1,0:T(8,128)S(1)} %add.6), channel_id=1, source_target_pairs={{0,7},{1,0},{2,1},{3,2},{4,3},{5,4},{6,5},{7,6},{8,15},{9,8},{10,9... | collective-permute-start | bytes 294920 | tf_op jit(solution)/shard_map/ppermute | solution.py:381
